TPU v7x, 512 devices: a whole 4x8x8 slice. The times are simulated.
512 devices in a mesh: tm: 4 (over y_hi, core), slab: 8 (over z), coarse: 16 (over x, y_lo).
Axes of the slice: x: 4, y: 8 (y_hi: 2, y_lo: 4; y = y_hi * 4 + y_lo), z: 8, core: 2. Of those that a mesh axis runs over, the one named last changes fastest.
Arguments:
- states: float32 [4, 32, 256, 256], P('tm', 'slab', 'coarse'), may hold values from -6 to 6
- diffusivity: float32 [32, 256, 256], P('slab', 'coarse'), may hold values from 0.25 to 2
- velocity: float32 [3, 32, 256, 256], P(None, 'slab', 'coarse'), may hold values from -0.5 to 0.5
Outputs:
- new_states: float32 [4, 32, 256, 256], P('tm', 'slab', 'coarse')
All inputs are finite; a program needn't handle non-finite values.
Results may differ from a plain program's by a relative error of at most 0.0001.
Values sent between devices are 32-bit elements; how exact they have to be, the bound alone decides.
A program may use at most 64 MiB of HBM per device.

v0:
```python
import jax
import jax.numpy as jnp
from jax import lax
from jax.sharding import PartitionSpec as P

SECTIONS = 4
FINE_STEPS = 2


fine_step = 1.0
relaxation = 0.8


def extended(block, sides, width):
    for axis, dim in sides:
        count = lax.axis_size(axis)
        forward = [(i, i + 1) for i in range(count - 1)]
        backward = [(target, source) for source, target in forward]
        low = lax.ppermute(
            lax.slice_in_dim(block, block.shape[dim] - width, None, axis=dim), axis, forward
        )
        high = lax.ppermute(lax.slice_in_dim(block, 0, width, axis=dim), axis, backward)
        block = jnp.concatenate([low, block, high], axis=dim)
    return block


def passed_along(block, axis, distance):
    devices = range(lax.axis_size(axis))
    route = [(i - distance, i) for i in devices if i - distance in devices]
    return lax.ppermute(block, axis, route)


def chebyshev_coefficients(sections):
    damping = 0.05
    centre_point = 1.0 + damping / (sections * sections)
    chebyshev = [1.0, centre_point]
    slopes = [0.0, 1.0]
    for degree in range(2, sections + 1):
        chebyshev.append(2.0 * centre_point * chebyshev[degree - 1] - chebyshev[degree - 2])
        slopes.append(
            2.0 * chebyshev[degree - 1]
            + 2.0 * centre_point * slopes[degree - 1]
            - slopes[degree - 2]
        )
    slope_ratio = chebyshev[sections] / slopes[sections]
    weights = [1.0 / entry for entry in chebyshev]
    scales = [0.0, 0.0]
    carries = [0.0, 0.0]
    tildes = [0.0, slope_ratio / centre_point]
    for degree in range(2, sections + 1):
        scales.append(2.0 * weights[degree] * centre_point / weights[degree - 1])
        carries.append(-weights[degree] / weights[degree - 2])
        tildes.append(2.0 * weights[degree] * slope_ratio / weights[degree - 1])
    return (scales, carries, tildes)


def stencil(padded, coeffs, spacing):
    centre = padded[1:-1, 1:-1, 1:-1]
    depth_after = padded[2:, 1:-1, 1:-1]
    depth_before = padded[:-2, 1:-1, 1:-1]
    row_after = padded[1:-1, 2:, 1:-1]
    row_before = padded[1:-1, :-2, 1:-1]
    column_after = padded[1:-1, 1:-1, 2:]
    column_before = padded[1:-1, 1:-1, :-2]
    beside_all = depth_after + depth_before + row_after + row_before + column_after + column_before
    spread = coeffs[0] * (beside_all - 6.0 * centre) / (spacing * spacing)
    drifts = (
        coeffs[1] * (depth_after - depth_before)
        + coeffs[2] * (row_after - row_before)
        + coeffs[3] * (column_after - column_before)
    ) / (2.0 * spacing)
    return spread - drifts


def shrink(values):
    return values.reshape(
        values.shape[0] // 2, 2, values.shape[1] // 2, 2, values.shape[2] // 2, 2
    ).mean(axis=(1, 3, 5))


def expand(values):
    return jnp.repeat(jnp.repeat(jnp.repeat(values, 2, 0), 2, 1), 2, 2)


def pad_columns(values):
    return jnp.pad(values, ((0, 0), (0, 0), (1, 1)))


def solve_padding(values):
    return pad_columns(extended(values, (("slab", 0), ("coarse", 1)), 1))


def coarse_padding(values):
    return pad_columns(extended(values, (("slab", 0), ("coarse", 1)), 1))


def section_padding(values):
    return pad_columns(extended(values, (("slab", 0), ("coarse", 1)), 1))


def coarse_step(source, coeffs, coarse_coeffs):
    interval = FINE_STEPS * fine_step
    diagonal = 1.0 + 6.0 * interval * coeffs[0]

    def misfit(trial):
        return source - (trial - interval * stencil(solve_padding(trial), coeffs, 1.0))

    smoothed = source + relaxation * misfit(source) / diagonal
    coarse_source = shrink(misfit(smoothed))
    coarse_diagonal = 1.0 + 6.0 * interval * coarse_coeffs[0] / 4.0
    guess_one = relaxation * coarse_source / coarse_diagonal
    coarse_misfit = coarse_source - (
        guess_one - interval * stencil(coarse_padding(guess_one), coarse_coeffs, 2.0)
    )
    guess_two = guess_one + relaxation * coarse_misfit / coarse_diagonal
    second = smoothed + expand(guess_two)
    return second + relaxation * misfit(second) / diagonal


def fine_thin(start_field, coeffs):
    scales, carries, tildes = chebyshev_coefficients(SECTIONS)
    for repeat in range(FINE_STEPS):
        before = start_field
        current = start_field + tildes[1] * fine_step * stencil(
            section_padding(start_field), coeffs, 1.0
        )
        for degree in range(2, SECTIONS + 1):
            update = (
                scales[degree] * current
                + carries[degree] * before
                + tildes[degree] * fine_step * stencil(section_padding(current), coeffs, 1.0)
            )
            before, current = (current, update)
        start_field = current
    return start_field


def per_device(states, diffusivity, velocity):
    coeffs = jnp.concatenate([diffusivity[None], velocity], 0)
    coarse_coeffs = jnp.stack([shrink(coeffs[number]) for number in range(4)])
    own_start = states[0]
    fine_end = fine_thin(own_start, coeffs)
    coarse_old = coarse_step(own_start, coeffs, coarse_coeffs)
    corrections = fine_end - coarse_old
    position = lax.axis_index("tm")
    window_count = lax.axis_size("tm")
    current = coarse_old + corrections
    result = current
    for turn_number in range(1, window_count):
        incoming = passed_along(current, "tm", 1)
        current = coarse_step(incoming, coeffs, coarse_coeffs) + corrections
        result = jnp.where(position == turn_number, current, result)
    return result[None]


def solution(mesh):
    return jax.shard_map(
        per_device,
        mesh=mesh,
        in_specs=(
            P("tm", "slab", "coarse", None),
            P("slab", "coarse", None),
            P(None, "slab", "coarse", None),
        ),
        out_specs=P("tm", "slab", "coarse", None),
        check_vma=False,
    )
```

profile of v0, /device:TPU:226, one launch (start us, length us, event | category | flops | bytes accessed | tf_op | source)
XLA Modules:
  0.0 527.5 jit_solution(11758566556081209717)
XLA Ops:
  2.7 5.5 %collective-permute-start.1 = (f32[1,16,256]{2,1,0:T(8,128)S(1)}, f32[1,16,256]{2,1,0:T(8,128)S(1)}, u32[]{:S(2)}, u32[]{:S(2)}) collective-permute-start(f32[1,16,256]{2,1,0:T(8,128)S(1)} %get-tuple-element.86), channel_id=1, source_target_pairs={{0,16},{16,32},{32,48},{48,64},{64,80},{80,96},{96,112},{1,17},{17... | collective-permute-start | bytes 49160 | tf_op jit(solution)/shard_map/ppermute | solution.py:19
  16.2 5.1 collective-permute-done.3
  25.6 5.4 %collective-permute-start.17 = (f32[1,16,256]{2,1,0:T(8,128)S(1)}, f32[1,16,256]{2,1,0:T(8,128)S(1)}, u32[]{:S(2)}, u32[]{:S(2)}) collective-permute-start(f32[1,16,256]{2,1,0:T(8,128)S(1)} %get-tuple-element.80), channel_id=1, source_target_pairs={{0,16},{16,32},{32,48},{48,64},{64,80},{80,96},{96,112},{1,17},{17... | collective-permute-start | bytes 49160 | tf_op jit(solution)/shard_map/ppermute | solution.py:19
  31.9 6.3 %reshape_squeeze_broadcast_in_dim.3 = f32[2,2,8,2,128,2]{5,4,3,2,1,0:T(8,128)} reshape(f32[4,16,256]{2,1,0:T(8,128)} %param.4) | data formatting | bytes 131072 | tf_op jit(solution)/shard_map/reshape;squeeze;broadcast_in_dim | solution.py:76
  38.2 5.6 %reshape_squeeze.9 = f32[2,2,8,2,128,2]{5,4,3,2,1,0:T(8,128)} reshape(f32[1,4,16,256]{3,2,1,0:T(8,128)S(1)} %get-tuple-element.9) | data formatting | bytes 131072 | tf_op jit(solution)/shard_map/reshape;squeeze | solution.py:76
  48.9 5.5 %reshape_squeeze.10 = f32[2,2,8,2,128,2]{5,4,3,2,1,0:T(8,128)} reshape(f32[1,4,16,256]{3,2,1,0:T(8,128)S(1)} %get-tuple-element.11) | data formatting | bytes 131072 | tf_op jit(solution)/shard_map/reshape;squeeze | solution.py:76
  57.0 5.5 %reshape_squeeze.11 = f32[2,2,8,2,128,2]{5,4,3,2,1,0:T(8,128)} reshape(f32[1,4,16,256]{3,2,1,0:T(8,128)S(1)} %get-tuple-element.10) | data formatting | bytes 131072 | tf_op jit(solution)/shard_map/reshape;squeeze | solution.py:76
  77.5 5.1 collective-permute-start.21
  84.6 5.1 collective-permute-start.5
  95.7 4.6 collective-permute-start.6
  104.5 5.1 collective-permute-start.25
  111.0 6.6 %collective-permute-start.26 = (f32[6,1,256]{2,1,0:T(1,128)S(1)}, f32[6,1,256]{2,1,0:T(1,128)S(1)}, u32[]{:S(2)}, u32[]{:S(2)}) collective-permute-start(f32[6,1,256]{2,1,0:T(1,128)S(1)} %get-tuple-element.39), channel_id=1, source_target_pairs={{1,0},{2,1},{3,2},{4,3},{5,4},{6,5},{7,6},{8,7},{9,8},{10,9},{11,1... | collective-permute-start | bytes 18440 | tf_op jit(solution)/shard_map/ppermute | solution.py:22
  119.7 5.5 %reshape.50 = f32[2,2,8,2,128,2]{5,4,3,2,1,0:T(8,128)} reshape(f32[4,16,256]{2,1,0:T(8,128)S(1)} %fusion.21) | data formatting | bytes 131072 | tf_op jit(solution)/shard_map/reshape | solution.py:76
  130.0 5.4 %collective-permute-start.29 = (f32[1,16,256]{2,1,0:T(8,128)S(1)}, f32[1,16,256]{2,1,0:T(8,128)S(1)}, u32[]{:S(2)}, u32[]{:S(2)}) collective-permute-start(f32[1,16,256]{2,1,0:T(8,128)S(1)} %get-tuple-element.74), channel_id=1, source_target_pairs={{0,16},{16,32},{32,48},{48,64},{64,80},{80,96},{96,112},{1,17},{17... | collective-permute-start | bytes 49160 | tf_op jit(solution)/shard_map/ppermute | solution.py:19
  136.9 6.6 %collective-permute-start.30 = (f32[6,1,256]{2,1,0:T(1,128)S(1)}, f32[6,1,256]{2,1,0:T(1,128)S(1)}, u32[]{:S(2)}, u32[]{:S(2)}) collective-permute-start(f32[6,1,256]{2,1,0:T(1,128)S(1)} %get-tuple-element.37), channel_id=1, source_target_pairs={{1,0},{2,1},{3,2},{4,3},{5,4},{6,5},{7,6},{8,7},{9,8},{10,9},{11,1... | collective-permute-start | bytes 18440 | tf_op jit(solution)/shard_map/ppermute | solution.py:22
  147.4 5.4 %collective-permute-start.9 = (f32[1,8,128]{2,1,0:T(8,128)S(1)}, f32[1,8,128]{2,1,0:T(8,128)S(1)}, u32[]{:S(2)}, u32[]{:S(2)}) collective-permute-start(f32[1,8,128]{2,1,0:T(8,128)S(1)} %get-tuple-element.102), channel_id=1, source_target_pairs={{0,16},{16,32},{32,48},{48,64},{64,80},{80,96},{96,112},{1,17},{17... | collective-permute-start | bytes 12296 | tf_op jit(solution)/shard_map/ppermute | solution.py:19
  155.1 5.1 collective-permute-start.33
  160.2 6.6 %collective-permute-start.10 = (f32[4,1,128]{2,1,0:T(1,128)S(1)}, f32[4,1,128]{2,1,0:T(1,128)S(1)}, u32[]{:S(2)}, u32[]{:S(2)}) collective-permute-start(f32[4,1,128]{2,1,0:T(1,128)S(1)} %get-tuple-element.95), channel_id=1, source_target_pairs={{1,0},{2,1},{3,2},{4,3},{5,4},{6,5},{7,6},{8,7},{9,8},{10,9},{11,1... | collective-permute-start | bytes 6152 | tf_op jit(solution)/shard_map/ppermute | solution.py:22
  168.8 6.6 %collective-permute-start.34 = (f32[6,1,256]{2,1,0:T(1,128)S(1)}, f32[6,1,256]{2,1,0:T(1,128)S(1)}, u32[]{:S(2)}, u32[]{:S(2)}) collective-permute-start(f32[6,1,256]{2,1,0:T(1,128)S(1)} %get-tuple-element.35), channel_id=1, source_target_pairs={{1,0},{2,1},{3,2},{4,3},{5,4},{6,5},{7,6},{8,7},{9,8},{10,9},{11,1... | collective-permute-start | bytes 18440 | tf_op jit(solution)/shard_map/ppermute | solution.py:22
  177.5 6.2 %collective-permute-done.35 = f32[6,1,256]{2,1,0:T(1,128)S(1)} collective-permute-done((f32[6,1,256]{2,1,0:T(1,128)S(1)}, f32[6,1,256]{2,1,0:T(1,128)S(1)}, u32[]{:S(2)}, u32[]{:S(2)}) %collective-permute-start.35) | collective-permute-done | bytes 6176 | tf_op jit(solution)/shard_map/ppermute | solution.py:19
  186.1 5.1 collective-permute-start.37
  200.5 5.4 %collective-permute-start.13 = (f32[1,16,256]{2,1,0:T(8,128)S(1)}, f32[1,16,256]{2,1,0:T(8,128)S(1)}, u32[]{:S(2)}, u32[]{:S(2)}) collective-permute-start(f32[1,16,256]{2,1,0:T(8,128)S(1)} %get-tuple-element.82), channel_id=1, source_target_pairs={{0,16},{16,32},{32,48},{48,64},{64,80},{80,96},{96,112},{1,17},{17... | collective-permute-start | bytes 49160 | tf_op jit(solution)/shard_map/ppermute | solution.py:19
  208.1 5.1 collective-permute-start.41
  213.3 4.6 collective-permute-start.14
  219.9 6.6 %collective-permute-start.42 = (f32[6,1,256]{2,1,0:T(1,128)S(1)}, f32[6,1,256]{2,1,0:T(1,128)S(1)}, u32[]{:S(2)}, u32[]{:S(2)}) collective-permute-start(f32[6,1,256]{2,1,0:T(1,128)S(1)} %get-tuple-element.31), channel_id=1, source_target_pairs={{1,0},{2,1},{3,2},{4,3},{5,4},{6,5},{7,6},{8,7},{9,8},{10,9},{11,1... | collective-permute-start | bytes 18440 | tf_op jit(solution)/shard_map/ppermute | solution.py:22
  228.6 6.1 %collective-permute-done.43 = f32[6,1,256]{2,1,0:T(1,128)S(1)} collective-permute-done((f32[6,1,256]{2,1,0:T(1,128)S(1)}, f32[6,1,256]{2,1,0:T(1,128)S(1)}, u32[]{:S(2)}, u32[]{:S(2)}) %collective-permute-start.43) | collective-permute-done | bytes 6176 | tf_op jit(solution)/shard_map/ppermute | solution.py:19
  237.0 7.6 %collective-permute-done.44 = f32[4,16,256]{2,1,0:T(8,128)S(1)} collective-permute-done((f32[4,16,256]{2,1,0:T(8,128)S(1)}, f32[4,16,256]{2,1,0:T(8,128)S(1)}, u32[]{:S(2)}, u32[]{:S(2)}) %collective-permute-start.44) | collective-permute-done | bytes 65568 | tf_op jit(solution)/shard_map/ppermute | solution.py:30
  260.0 4.3 collective-permute-done.48
  266.6 5.1 collective-permute-start.50
  283.6 5.5 %reshape.54 = f32[2,2,8,2,128,2]{5,4,3,2,1,0:T(8,128)} reshape(f32[4,16,256]{2,1,0:T(8,128)S(1)} %fusion.76) | data formatting | bytes 131072 | tf_op jit(solution)/shard_map/reshape | solution.py:76
  293.6 5.4 %collective-permute-start.54 = (f32[1,8,128]{2,1,0:T(8,128)S(1)}, f32[1,8,128]{2,1,0:T(8,128)S(1)}, u32[]{:S(2)}, u32[]{:S(2)}) collective-permute-start(f32[1,8,128]{2,1,0:T(8,128)S(1)} %get-tuple-element.100), channel_id=1, source_target_pairs={{0,16},{16,32},{32,48},{48,64},{64,80},{80,96},{96,112},{1,17},{17... | collective-permute-start | bytes 12296 | tf_op jit(solution)/shard_map/ppermute | solution.py:19
  313.1 5.4 %collective-permute-start.58 = (f32[1,16,256]{2,1,0:T(8,128)S(1)}, f32[1,16,256]{2,1,0:T(8,128)S(1)}, u32[]{:S(2)}, u32[]{:S(2)}) collective-permute-start(f32[1,16,256]{2,1,0:T(8,128)S(1)} %get-tuple-element.62), channel_id=1, source_target_pairs={{0,16},{16,32},{32,48},{48,64},{64,80},{80,96},{96,112},{1,17},{17... | collective-permute-start | bytes 49160 | tf_op jit(solution)/shard_map/ppermute | solution.py:19
  325.8 4.5 collective-permute-done.60
  332.5 7.6 %collective-permute-done.61 = f32[4,16,256]{2,1,0:T(8,128)S(1)} collective-permute-done((f32[4,16,256]{2,1,0:T(8,128)S(1)}, f32[4,16,256]{2,1,0:T(8,128)S(1)}, u32[]{:S(2)}, u32[]{:S(2)}) %collective-permute-start.61) | collective-permute-done | bytes 65568 | tf_op jit(solution)/shard_map/ppermute | solution.py:30
  340.1 5.5 %collective-permute-start.63 = (f32[1,16,256]{2,1,0:T(8,128)S(1)}, f32[1,16,256]{2,1,0:T(8,128)S(1)}, u32[]{:S(2)}, u32[]{:S(2)}) collective-permute-start(f32[1,16,256]{2,1,0:T(8,128)S(1)} %get-tuple-element.61), channel_id=1, source_target_pairs={{0,16},{16,32},{32,48},{48,64},{64,80},{80,96},{96,112},{1,17},{17... | collective-permute-start | bytes 49160 | tf_op jit(solution)/shard_map/ppermute | solution.py:19
  347.5 4.9 collective-permute-done.62
  364.8 5.1 collective-permute-start.67
  381.8 5.5 %reshape.58 = f32[2,2,8,2,128,2]{5,4,3,2,1,0:T(8,128)} reshape(f32[4,16,256]{2,1,0:T(8,128)S(1)} %fusion.96) | data formatting | bytes 131072 | tf_op jit(solution)/shard_map/reshape | solution.py:76
  391.9 5.4 %collective-permute-start.71 = (f32[1,8,128]{2,1,0:T(8,128)S(1)}, f32[1,8,128]{2,1,0:T(8,128)S(1)}, u32[]{:S(2)}, u32[]{:S(2)}) collective-permute-start(f32[1,8,128]{2,1,0:T(8,128)S(1)} %get-tuple-element.98), channel_id=1, source_target_pairs={{0,16},{16,32},{32,48},{48,64},{64,80},{80,96},{96,112},{1,17},{17... | collective-permute-start | bytes 12296 | tf_op jit(solution)/shard_map/ppermute | solution.py:19
  411.4 5.4 %collective-permute-start.75 = (f32[1,16,256]{2,1,0:T(8,128)S(1)}, f32[1,16,256]{2,1,0:T(8,128)S(1)}, u32[]{:S(2)}, u32[]{:S(2)}) collective-permute-start(f32[1,16,256]{2,1,0:T(8,128)S(1)} %get-tuple-element.56), channel_id=1, source_target_pairs={{0,16},{16,32},{32,48},{48,64},{64,80},{80,96},{96,112},{1,17},{17... | collective-permute-start | bytes 49160 | tf_op jit(solution)/shard_map/ppermute | solution.py:19
  424.1 4.4 collective-permute-done.77
  430.7 7.6 %collective-permute-done.78 = f32[4,16,256]{2,1,0:T(8,128)S(1)} collective-permute-done((f32[4,16,256]{2,1,0:T(8,128)S(1)}, f32[4,16,256]{2,1,0:T(8,128)S(1)}, u32[]{:S(2)}, u32[]{:S(2)}) %collective-permute-start.78) | collective-permute-done | bytes 65568 | tf_op jit(solution)/shard_map/ppermute | solution.py:30
  438.3 5.5 %collective-permute-start.80 = (f32[1,16,256]{2,1,0:T(8,128)S(1)}, f32[1,16,256]{2,1,0:T(8,128)S(1)}, u32[]{:S(2)}, u32[]{:S(2)}) collective-permute-start(f32[1,16,256]{2,1,0:T(8,128)S(1)} %get-tuple-element.55), channel_id=1, source_target_pairs={{0,16},{16,32},{32,48},{48,64},{64,80},{80,96},{96,112},{1,17},{17... | collective-permute-start | bytes 49160 | tf_op jit(solution)/shard_map/ppermute | solution.py:19
  445.7 4.9 collective-permute-done.79
  463.0 5.1 collective-permute-start.84
  480.0 5.5 %reshape.62 = f32[2,2,8,2,128,2]{5,4,3,2,1,0:T(8,128)} reshape(f32[4,16,256]{2,1,0:T(8,128)S(1)} %fusion.116) | data formatting | bytes 131072 | tf_op jit(solution)/shard_map/reshape | solution.py:76
  490.1 5.4 %collective-permute-start.88 = (f32[1,8,128]{2,1,0:T(8,128)S(1)}, f32[1,8,128]{2,1,0:T(8,128)S(1)}, u32[]{:S(2)}, u32[]{:S(2)}) collective-permute-start(f32[1,8,128]{2,1,0:T(8,128)S(1)} %get-tuple-element.96), channel_id=1, source_target_pairs={{0,16},{16,32},{32,48},{48,64},{64,80},{80,96},{96,112},{1,17},{17... | collective-permute-start | bytes 12296 | tf_op jit(solution)/shard_map/ppermute | solution.py:19
  509.6 5.4 %collective-permute-start.92 = (f32[1,16,256]{2,1,0:T(8,128)S(1)}, f32[1,16,256]{2,1,0:T(8,128)S(1)}, u32[]{:S(2)}, u32[]{:S(2)}) collective-permute-start(f32[1,16,256]{2,1,0:T(8,128)S(1)} %get-tuple-element.50), channel_id=1, source_target_pairs={{0,16},{16,32},{32,48},{48,64},{64,80},{80,96},{96,112},{1,17},{17... | collective-permute-start | bytes 49160 | tf_op jit(solution)/shard_map/ppermute | solution.py:19
  (294 shorter events, 258.3 us)
Async XLA Ops:
  13.2 8.2 %collective-permute-start.3 = (f32[6,1,256]{2,1,0:T(1,128)S(1)}, f32[6,1,256]{2,1,0:T(1,128)S(1)}, u32[]{:S(2)}, u32[]{:S(2)}) collective-permute-start(f32[6,1,256]{2,1,0:T(1,128)S(1)} %get-tuple-element.48), channel_id=1, source_target_pairs={{0,1},{1,2},{2,3},{3,4},{4,5},{5,6},{6,7},{7,8},{8,9},{9,10},{10,1... | collective-permute-start | bytes 18440 | tf_op jit(solution)/shard_map/ppermute | solution.py:19
  23.7 41.4 %collective-permute-start.16 = (f32[1,16,256]{2,1,0:T(8,128)S(1)}, f32[1,16,256]{2,1,0:T(8,128)S(1)}, u32[]{:S(2)}, u32[]{:S(2)}) collective-permute-start(f32[1,16,256]{2,1,0:T(8,128)S(1)} %get-tuple-element.81), channel_id=1, source_target_pairs={{16,0},{32,16},{48,32},{64,48},{80,64},{96,80},{112,96},{17,1},{33... | collective-permute-start | bytes 49160 | tf_op jit(solution)/shard_map/ppermute | solution.py:22
  25.6 39.5 %collective-permute-start.17 = (f32[1,16,256]{2,1,0:T(8,128)S(1)}, f32[1,16,256]{2,1,0:T(8,128)S(1)}, u32[]{:S(2)}, u32[]{:S(2)}) collective-permute-start(f32[1,16,256]{2,1,0:T(8,128)S(1)} %get-tuple-element.80), channel_id=1, source_target_pairs={{0,16},{16,32},{32,48},{48,64},{64,80},{80,96},{96,112},{1,17},{17... | collective-permute-start | bytes 49160 | tf_op jit(solution)/shard_map/ppermute | solution.py:19
  67.1 8.2 %collective-permute-start.19 = (f32[6,1,256]{2,1,0:T(1,128)S(1)}, f32[6,1,256]{2,1,0:T(1,128)S(1)}, u32[]{:S(2)}, u32[]{:S(2)}) collective-permute-start(f32[6,1,256]{2,1,0:T(1,128)S(1)} %get-tuple-element.42), channel_id=1, source_target_pairs={{0,1},{1,2},{2,3},{3,4},{4,5},{5,6},{6,7},{7,8},{8,9},{9,10},{10,1... | collective-permute-start | bytes 18440 | tf_op jit(solution)/shard_map/ppermute | solution.py:19
  75.6 14.2 %collective-permute-start.20 = (f32[1,16,256]{2,1,0:T(8,128)S(1)}, f32[1,16,256]{2,1,0:T(8,128)S(1)}, u32[]{:S(2)}, u32[]{:S(2)}) collective-permute-start(f32[1,16,256]{2,1,0:T(8,128)S(1)} %get-tuple-element.79), channel_id=1, source_target_pairs={{16,0},{32,16},{48,32},{64,48},{80,64},{96,80},{112,96},{17,1},{33... | collective-permute-start | bytes 49160 | tf_op jit(solution)/shard_map/ppermute | solution.py:22
  77.5 12.2 %collective-permute-start.21 = (f32[1,16,256]{2,1,0:T(8,128)S(1)}, f32[1,16,256]{2,1,0:T(8,128)S(1)}, u32[]{:S(2)}, u32[]{:S(2)}) collective-permute-start(f32[1,16,256]{2,1,0:T(8,128)S(1)} %get-tuple-element.78), channel_id=1, source_target_pairs={{0,16},{16,32},{32,48},{48,64},{64,80},{80,96},{96,112},{1,17},{17... | collective-permute-start | bytes 49160 | tf_op jit(solution)/shard_map/ppermute | solution.py:19
  82.7 13.0 %collective-permute-start.4 = (f32[1,16,256]{2,1,0:T(8,128)S(1)}, f32[1,16,256]{2,1,0:T(8,128)S(1)}, u32[]{:S(2)}, u32[]{:S(2)}) collective-permute-start(f32[1,16,256]{2,1,0:T(8,128)S(1)} %get-tuple-element.85), channel_id=1, source_target_pairs={{16,0},{32,16},{48,32},{64,48},{80,64},{96,80},{112,96},{17,1},{33... | collective-permute-start | bytes 49160 | tf_op jit(solution)/shard_map/ppermute | solution.py:22
  84.6 11.1 %collective-permute-start.5 = (f32[1,16,256]{2,1,0:T(8,128)S(1)}, f32[1,16,256]{2,1,0:T(8,128)S(1)}, u32[]{:S(2)}, u32[]{:S(2)}) collective-permute-start(f32[1,16,256]{2,1,0:T(8,128)S(1)} %get-tuple-element.84), channel_id=1, source_target_pairs={{0,16},{16,32},{32,48},{48,64},{64,80},{80,96},{96,112},{1,17},{17... | collective-permute-start | bytes 49160 | tf_op jit(solution)/shard_map/ppermute | solution.py:19
  89.8 12.5 %collective-permute-start.22 = (f32[6,1,256]{2,1,0:T(1,128)S(1)}, f32[6,1,256]{2,1,0:T(1,128)S(1)}, u32[]{:S(2)}, u32[]{:S(2)}) collective-permute-start(f32[6,1,256]{2,1,0:T(1,128)S(1)} %get-tuple-element.41), channel_id=1, source_target_pairs={{1,0},{2,1},{3,2},{4,3},{5,4},{6,5},{7,6},{8,7},{9,8},{10,9},{11,1... | collective-permute-start | bytes 18440 | tf_op jit(solution)/shard_map/ppermute | solution.py:22
  91.7 10.5 %collective-permute-start.23 = (f32[6,1,256]{2,1,0:T(1,128)S(1)}, f32[6,1,256]{2,1,0:T(1,128)S(1)}, u32[]{:S(2)}, u32[]{:S(2)}) collective-permute-start(f32[6,1,256]{2,1,0:T(1,128)S(1)} %get-tuple-element.40), channel_id=1, source_target_pairs={{0,1},{1,2},{2,3},{3,4},{4,5},{5,6},{6,7},{7,8},{8,9},{9,10},{10,1... | collective-permute-start | bytes 18440 | tf_op jit(solution)/shard_map/ppermute | solution.py:19
  95.7 13.9 %collective-permute-start.6 = (f32[6,1,256]{2,1,0:T(1,128)S(1)}, f32[6,1,256]{2,1,0:T(1,128)S(1)}, u32[]{:S(2)}, u32[]{:S(2)}) collective-permute-start(f32[6,1,256]{2,1,0:T(1,128)S(1)} %get-tuple-element.47), channel_id=1, source_target_pairs={{1,0},{2,1},{3,2},{4,3},{5,4},{6,5},{7,6},{8,7},{9,8},{10,9},{11,1... | collective-permute-start | bytes 18440 | tf_op jit(solution)/shard_map/ppermute | solution.py:22
  100.3 9.3 %collective-permute-start.7 = (f32[6,1,256]{2,1,0:T(1,128)S(1)}, f32[6,1,256]{2,1,0:T(1,128)S(1)}, u32[]{:S(2)}, u32[]{:S(2)}) collective-permute-start(f32[6,1,256]{2,1,0:T(1,128)S(1)} %get-tuple-element.46), channel_id=1, source_target_pairs={{0,1},{1,2},{2,3},{3,4},{4,5},{5,6},{6,7},{7,8},{8,9},{9,10},{10,1... | collective-permute-start | bytes 18440 | tf_op jit(solution)/shard_map/ppermute | solution.py:19
  111.0 16.8 %collective-permute-start.26 = (f32[6,1,256]{2,1,0:T(1,128)S(1)}, f32[6,1,256]{2,1,0:T(1,128)S(1)}, u32[]{:S(2)}, u32[]{:S(2)}) collective-permute-start(f32[6,1,256]{2,1,0:T(1,128)S(1)} %get-tuple-element.39), channel_id=1, source_target_pairs={{1,0},{2,1},{3,2},{4,3},{5,4},{6,5},{7,6},{8,7},{9,8},{10,9},{11,1... | collective-permute-start | bytes 18440 | tf_op jit(solution)/shard_map/ppermute | solution.py:22
  117.7 10.1 %collective-permute-start.27 = (f32[6,1,256]{2,1,0:T(1,128)S(1)}, f32[6,1,256]{2,1,0:T(1,128)S(1)}, u32[]{:S(2)}, u32[]{:S(2)}) collective-permute-start(f32[6,1,256]{2,1,0:T(1,128)S(1)} %get-tuple-element.38), channel_id=1, source_target_pairs={{0,1},{1,2},{2,3},{3,4},{4,5},{5,6},{6,7},{7,8},{8,9},{9,10},{10,1... | collective-permute-start | bytes 18440 | tf_op jit(solution)/shard_map/ppermute | solution.py:19
  136.9 15.9 %collective-permute-start.30 = (f32[6,1,256]{2,1,0:T(1,128)S(1)}, f32[6,1,256]{2,1,0:T(1,128)S(1)}, u32[]{:S(2)}, u32[]{:S(2)}) collective-permute-start(f32[6,1,256]{2,1,0:T(1,128)S(1)} %get-tuple-element.37), channel_id=1, source_target_pairs={{1,0},{2,1},{3,2},{4,3},{5,4},{6,5},{7,6},{8,7},{9,8},{10,9},{11,1... | collective-permute-start | bytes 18440 | tf_op jit(solution)/shard_map/ppermute | solution.py:22
  143.5 9.3 %collective-permute-start.31 = (f32[6,1,256]{2,1,0:T(1,128)S(1)}, f32[6,1,256]{2,1,0:T(1,128)S(1)}, u32[]{:S(2)}, u32[]{:S(2)}) collective-permute-start(f32[6,1,256]{2,1,0:T(1,128)S(1)} %get-tuple-element.36), channel_id=1, source_target_pairs={{0,1},{1,2},{2,3},{3,4},{4,5},{5,6},{6,7},{7,8},{8,9},{9,10},{10,1... | collective-permute-start | bytes 18440 | tf_op jit(solution)/shard_map/ppermute | solution.py:19
  145.5 14.7 %collective-permute-start.8 = (f32[1,8,128]{2,1,0:T(8,128)S(1)}, f32[1,8,128]{2,1,0:T(8,128)S(1)}, u32[]{:S(2)}, u32[]{:S(2)}) collective-permute-start(f32[1,8,128]{2,1,0:T(8,128)S(1)} %get-tuple-element.103), channel_id=1, source_target_pairs={{16,0},{32,16},{48,32},{64,48},{80,64},{96,80},{112,96},{17,1},{33... | collective-permute-start | bytes 12296 | tf_op jit(solution)/shard_map/ppermute | solution.py:22
  147.4 12.8 %collective-permute-start.9 = (f32[1,8,128]{2,1,0:T(8,128)S(1)}, f32[1,8,128]{2,1,0:T(8,128)S(1)}, u32[]{:S(2)}, u32[]{:S(2)}) collective-permute-start(f32[1,8,128]{2,1,0:T(8,128)S(1)} %get-tuple-element.102), channel_id=1, source_target_pairs={{0,16},{16,32},{32,48},{48,64},{64,80},{80,96},{96,112},{1,17},{17... | collective-permute-start | bytes 12296 | tf_op jit(solution)/shard_map/ppermute | solution.py:19
  153.1 15.7 %collective-permute-start.32 = (f32[1,16,256]{2,1,0:T(8,128)S(1)}, f32[1,16,256]{2,1,0:T(8,128)S(1)}, u32[]{:S(2)}, u32[]{:S(2)}) collective-permute-start(f32[1,16,256]{2,1,0:T(8,128)S(1)} %get-tuple-element.73), channel_id=1, source_target_pairs={{16,0},{32,16},{48,32},{64,48},{80,64},{96,80},{112,96},{17,1},{33... | collective-permute-start | bytes 49160 | tf_op jit(solution)/shard_map/ppermute | solution.py:22
  155.1 13.7 %collective-permute-start.33 = (f32[1,16,256]{2,1,0:T(8,128)S(1)}, f32[1,16,256]{2,1,0:T(8,128)S(1)}, u32[]{:S(2)}, u32[]{:S(2)}) collective-permute-start(f32[1,16,256]{2,1,0:T(8,128)S(1)} %get-tuple-element.72), channel_id=1, source_target_pairs={{0,16},{16,32},{32,48},{48,64},{64,80},{80,96},{96,112},{1,17},{17... | collective-permute-start | bytes 49160 | tf_op jit(solution)/shard_map/ppermute | solution.py:19
  160.2 17.2 %collective-permute-start.10 = (f32[4,1,128]{2,1,0:T(1,128)S(1)}, f32[4,1,128]{2,1,0:T(1,128)S(1)}, u32[]{:S(2)}, u32[]{:S(2)}) collective-permute-start(f32[4,1,128]{2,1,0:T(1,128)S(1)} %get-tuple-element.95), channel_id=1, source_target_pairs={{1,0},{2,1},{3,2},{4,3},{5,4},{6,5},{7,6},{8,7},{9,8},{10,9},{11,1... | collective-permute-start | bytes 6152 | tf_op jit(solution)/shard_map/ppermute | solution.py:22
  166.9 10.5 %collective-permute-start.11 = (f32[4,1,128]{2,1,0:T(1,128)S(1)}, f32[4,1,128]{2,1,0:T(1,128)S(1)}, u32[]{:S(2)}, u32[]{:S(2)}) collective-permute-start(f32[4,1,128]{2,1,0:T(1,128)S(1)} %get-tuple-element.94), channel_id=1, source_target_pairs={{0,1},{1,2},{2,3},{3,4},{4,5},{5,6},{6,7},{7,8},{8,9},{9,10},{10,1... | collective-permute-start | bytes 6152 | tf_op jit(solution)/shard_map/ppermute | solution.py:19
  168.8 8.7 %collective-permute-start.34 = (f32[6,1,256]{2,1,0:T(1,128)S(1)}, f32[6,1,256]{2,1,0:T(1,128)S(1)}, u32[]{:S(2)}, u32[]{:S(2)}) collective-permute-start(f32[6,1,256]{2,1,0:T(1,128)S(1)} %get-tuple-element.35), channel_id=1, source_target_pairs={{1,0},{2,1},{3,2},{4,3},{5,4},{6,5},{7,6},{8,7},{9,8},{10,9},{11,1... | collective-permute-start | bytes 18440 | tf_op jit(solution)/shard_map/ppermute | solution.py:22
  175.5 8.2 %collective-permute-start.35 = (f32[6,1,256]{2,1,0:T(1,128)S(1)}, f32[6,1,256]{2,1,0:T(1,128)S(1)}, u32[]{:S(2)}, u32[]{:S(2)}) collective-permute-start(f32[6,1,256]{2,1,0:T(1,128)S(1)} %get-tuple-element.34), channel_id=1, source_target_pairs={{0,1},{1,2},{2,3},{3,4},{4,5},{5,6},{6,7},{7,8},{8,9},{9,10},{10,1... | collective-permute-start | bytes 18440 | tf_op jit(solution)/shard_map/ppermute | solution.py:19
  192.7 13.2 %collective-permute-start.38 = (f32[6,1,256]{2,1,0:T(1,128)S(1)}, f32[6,1,256]{2,1,0:T(1,128)S(1)}, u32[]{:S(2)}, u32[]{:S(2)}) collective-permute-start(f32[6,1,256]{2,1,0:T(1,128)S(1)} %get-tuple-element.33), channel_id=1, source_target_pairs={{1,0},{2,1},{3,2},{4,3},{5,4},{6,5},{7,6},{8,7},{9,8},{10,9},{11,1... | collective-permute-start | bytes 18440 | tf_op jit(solution)/shard_map/ppermute | solution.py:22
  194.6 11.3 %collective-permute-start.39 = (f32[6,1,256]{2,1,0:T(1,128)S(1)}, f32[6,1,256]{2,1,0:T(1,128)S(1)}, u32[]{:S(2)}, u32[]{:S(2)}) collective-permute-start(f32[6,1,256]{2,1,0:T(1,128)S(1)} %get-tuple-element.32), channel_id=1, source_target_pairs={{0,1},{1,2},{2,3},{3,4},{4,5},{5,6},{6,7},{7,8},{8,9},{9,10},{10,1... | collective-permute-start | bytes 18440 | tf_op jit(solution)/shard_map/ppermute | solution.py:19
  198.5 14.7 %collective-permute-start.12 = (f32[1,16,256]{2,1,0:T(8,128)S(1)}, f32[1,16,256]{2,1,0:T(8,128)S(1)}, u32[]{:S(2)}, u32[]{:S(2)}) collective-permute-start(f32[1,16,256]{2,1,0:T(8,128)S(1)} %get-tuple-element.83), channel_id=1, source_target_pairs={{16,0},{32,16},{48,32},{64,48},{80,64},{96,80},{112,96},{17,1},{33... | collective-permute-start | bytes 49160 | tf_op jit(solution)/shard_map/ppermute | solution.py:22
  200.5 12.8 %collective-permute-start.13 = (f32[1,16,256]{2,1,0:T(8,128)S(1)}, f32[1,16,256]{2,1,0:T(8,128)S(1)}, u32[]{:S(2)}, u32[]{:S(2)}) collective-permute-start(f32[1,16,256]{2,1,0:T(8,128)S(1)} %get-tuple-element.82), channel_id=1, source_target_pairs={{0,16},{16,32},{32,48},{48,64},{64,80},{80,96},{96,112},{1,17},{17... | collective-permute-start | bytes 49160 | tf_op jit(solution)/shard_map/ppermute | solution.py:19
  206.2 13.7 %collective-permute-start.40 = (f32[1,16,256]{2,1,0:T(8,128)S(1)}, f32[1,16,256]{2,1,0:T(8,128)S(1)}, u32[]{:S(2)}, u32[]{:S(2)}) collective-permute-start(f32[1,16,256]{2,1,0:T(8,128)S(1)} %get-tuple-element.69), channel_id=1, source_target_pairs={{16,0},{32,16},{48,32},{64,48},{80,64},{96,80},{112,96},{17,1},{33... | collective-permute-start | bytes 49160 | tf_op jit(solution)/shard_map/ppermute | solution.py:22
  208.1 11.7 %collective-permute-start.41 = (f32[1,16,256]{2,1,0:T(8,128)S(1)}, f32[1,16,256]{2,1,0:T(8,128)S(1)}, u32[]{:S(2)}, u32[]{:S(2)}) collective-permute-start(f32[1,16,256]{2,1,0:T(8,128)S(1)} %get-tuple-element.68), channel_id=1, source_target_pairs={{0,16},{16,32},{32,48},{48,64},{64,80},{80,96},{96,112},{1,17},{17... | collective-permute-start | bytes 49160 | tf_op jit(solution)/shard_map/ppermute | solution.py:19
  213.3 15.2 %collective-permute-start.14 = (f32[6,1,256]{2,1,0:T(1,128)S(1)}, f32[6,1,256]{2,1,0:T(1,128)S(1)}, u32[]{:S(2)}, u32[]{:S(2)}) collective-permute-start(f32[6,1,256]{2,1,0:T(1,128)S(1)} %get-tuple-element.45), channel_id=1, source_target_pairs={{1,0},{2,1},{3,2},{4,3},{5,4},{6,5},{7,6},{8,7},{9,8},{10,9},{11,1... | collective-permute-start | bytes 18440 | tf_op jit(solution)/shard_map/ppermute | solution.py:22
  217.9 10.5 %collective-permute-start.15 = (f32[6,1,256]{2,1,0:T(1,128)S(1)}, f32[6,1,256]{2,1,0:T(1,128)S(1)}, u32[]{:S(2)}, u32[]{:S(2)}) collective-permute-start(f32[6,1,256]{2,1,0:T(1,128)S(1)} %get-tuple-element.44), channel_id=1, source_target_pairs={{0,1},{1,2},{2,3},{3,4},{4,5},{5,6},{6,7},{7,8},{8,9},{9,10},{10,1... | collective-permute-start | bytes 18440 | tf_op jit(solution)/shard_map/ppermute | solution.py:19
  219.9 8.7 %collective-permute-start.42 = (f32[6,1,256]{2,1,0:T(1,128)S(1)}, f32[6,1,256]{2,1,0:T(1,128)S(1)}, u32[]{:S(2)}, u32[]{:S(2)}) collective-permute-start(f32[6,1,256]{2,1,0:T(1,128)S(1)} %get-tuple-element.31), channel_id=1, source_target_pairs={{1,0},{2,1},{3,2},{4,3},{5,4},{6,5},{7,6},{8,7},{9,8},{10,9},{11,1... | collective-permute-start | bytes 18440 | tf_op jit(solution)/shard_map/ppermute | solution.py:22
  226.5 8.2 %collective-permute-start.43 = (f32[6,1,256]{2,1,0:T(1,128)S(1)}, f32[6,1,256]{2,1,0:T(1,128)S(1)}, u32[]{:S(2)}, u32[]{:S(2)}) collective-permute-start(f32[6,1,256]{2,1,0:T(1,128)S(1)} %get-tuple-element.30), channel_id=1, source_target_pairs={{0,1},{1,2},{2,3},{3,4},{4,5},{5,6},{6,7},{7,8},{8,9},{9,10},{10,1... | collective-permute-start | bytes 18440 | tf_op jit(solution)/shard_map/ppermute | solution.py:19
  235.1 9.5 %collective-permute-start.44 = (f32[4,16,256]{2,1,0:T(8,128)S(1)}, f32[4,16,256]{2,1,0:T(8,128)S(1)}, u32[]{:S(2)}, u32[]{:S(2)}) collective-permute-start(f32[4,16,256]{2,1,0:T(8,128)S(1)} %get-tuple-element.5), channel_id=1, source_target_pairs={{0,128},{128,256},{256,384},{1,129},{129,257},{257,385},{2,130},{1... | collective-permute-start | bytes 196616 | tf_op jit(solution)/shard_map/ppermute | solution.py:30
  256.1 8.2 %collective-permute-start.48 = (f32[6,1,256]{2,1,0:T(1,128)S(1)}, f32[6,1,256]{2,1,0:T(1,128)S(1)}, u32[]{:S(2)}, u32[]{:S(2)}) collective-permute-start(f32[6,1,256]{2,1,0:T(1,128)S(1)} %get-tuple-element.28), channel_id=1, source_target_pairs={{0,1},{1,2},{2,3},{3,4},{4,5},{5,6},{6,7},{7,8},{8,9},{9,10},{10,1... | collective-permute-start | bytes 18440 | tf_op jit(solution)/shard_map/ppermute | solution.py:19
  275.1 8.2 %collective-permute-start.52 = (f32[6,1,256]{2,1,0:T(1,128)S(1)}, f32[6,1,256]{2,1,0:T(1,128)S(1)}, u32[]{:S(2)}, u32[]{:S(2)}) collective-permute-start(f32[6,1,256]{2,1,0:T(1,128)S(1)} %get-tuple-element.26), channel_id=1, source_target_pairs={{0,1},{1,2},{2,3},{3,4},{4,5},{5,6},{6,7},{7,8},{8,9},{9,10},{10,1... | collective-permute-start | bytes 18440 | tf_op jit(solution)/shard_map/ppermute | solution.py:19
  302.3 8.2 %collective-permute-start.56 = (f32[4,1,128]{2,1,0:T(1,128)S(1)}, f32[4,1,128]{2,1,0:T(1,128)S(1)}, u32[]{:S(2)}, u32[]{:S(2)}) collective-permute-start(f32[4,1,128]{2,1,0:T(1,128)S(1)} %get-tuple-element.92), channel_id=1, source_target_pairs={{0,1},{1,2},{2,3},{3,4},{4,5},{5,6},{6,7},{7,8},{8,9},{9,10},{10,1... | collective-permute-start | bytes 6152 | tf_op jit(solution)/shard_map/ppermute | solution.py:19
  321.9 8.4 %collective-permute-start.60 = (f32[6,1,256]{2,1,0:T(1,128)S(1)}, f32[6,1,256]{2,1,0:T(1,128)S(1)}, u32[]{:S(2)}, u32[]{:S(2)}) collective-permute-start(f32[6,1,256]{2,1,0:T(1,128)S(1)} %get-tuple-element.24), channel_id=1, source_target_pairs={{0,1},{1,2},{2,3},{3,4},{4,5},{5,6},{6,7},{7,8},{8,9},{9,10},{10,1... | collective-permute-start | bytes 18440 | tf_op jit(solution)/shard_map/ppermute | solution.py:19
  330.6 9.5 %collective-permute-start.61 = (f32[4,16,256]{2,1,0:T(8,128)S(1)}, f32[4,16,256]{2,1,0:T(8,128)S(1)}, u32[]{:S(2)}, u32[]{:S(2)}) collective-permute-start(f32[4,16,256]{2,1,0:T(8,128)S(1)} %fusion.86), channel_id=1, source_target_pairs={{0,128},{128,256},{256,384},{1,129},{129,257},{257,385},{2,130},{1... | collective-permute-start | bytes 196616 | tf_op jit(solution)/shard_map/ppermute | solution.py:30
  354.4 8.2 %collective-permute-start.65 = (f32[6,1,256]{2,1,0:T(1,128)S(1)}, f32[6,1,256]{2,1,0:T(1,128)S(1)}, u32[]{:S(2)}, u32[]{:S(2)}) collective-permute-start(f32[6,1,256]{2,1,0:T(1,128)S(1)} %get-tuple-element.22), channel_id=1, source_target_pairs={{0,1},{1,2},{2,3},{3,4},{4,5},{5,6},{6,7},{7,8},{8,9},{9,10},{10,1... | collective-permute-start | bytes 18440 | tf_op jit(solution)/shard_map/ppermute | solution.py:19
  373.3 8.2 %collective-permute-start.69 = (f32[6,1,256]{2,1,0:T(1,128)S(1)}, f32[6,1,256]{2,1,0:T(1,128)S(1)}, u32[]{:S(2)}, u32[]{:S(2)}) collective-permute-start(f32[6,1,256]{2,1,0:T(1,128)S(1)} %get-tuple-element.20), channel_id=1, source_target_pairs={{0,1},{1,2},{2,3},{3,4},{4,5},{5,6},{6,7},{7,8},{8,9},{9,10},{10,1... | collective-permute-start | bytes 18440 | tf_op jit(solution)/shard_map/ppermute | solution.py:19
  400.5 8.2 %collective-permute-start.73 = (f32[4,1,128]{2,1,0:T(1,128)S(1)}, f32[4,1,128]{2,1,0:T(1,128)S(1)}, u32[]{:S(2)}, u32[]{:S(2)}) collective-permute-start(f32[4,1,128]{2,1,0:T(1,128)S(1)} %get-tuple-element.90), channel_id=1, source_target_pairs={{0,1},{1,2},{2,3},{3,4},{4,5},{5,6},{6,7},{7,8},{8,9},{9,10},{10,1... | collective-permute-start | bytes 6152 | tf_op jit(solution)/shard_map/ppermute | solution.py:19
  420.1 8.3 %collective-permute-start.77 = (f32[6,1,256]{2,1,0:T(1,128)S(1)}, f32[6,1,256]{2,1,0:T(1,128)S(1)}, u32[]{:S(2)}, u32[]{:S(2)}) collective-permute-start(f32[6,1,256]{2,1,0:T(1,128)S(1)} %get-tuple-element.18), channel_id=1, source_target_pairs={{0,1},{1,2},{2,3},{3,4},{4,5},{5,6},{6,7},{7,8},{8,9},{9,10},{10,1... | collective-permute-start | bytes 18440 | tf_op jit(solution)/shard_map/ppermute | solution.py:19
  428.8 9.5 %collective-permute-start.78 = (f32[4,16,256]{2,1,0:T(8,128)S(1)}, f32[4,16,256]{2,1,0:T(8,128)S(1)}, u32[]{:S(2)}, u32[]{:S(2)}) collective-permute-start(f32[4,16,256]{2,1,0:T(8,128)S(1)} %fusion.106), channel_id=1, source_target_pairs={{0,128},{128,256},{256,384},{1,129},{129,257},{257,385},{2,130},{1... | collective-permute-start | bytes 196616 | tf_op jit(solution)/shard_map/ppermute | solution.py:30
  452.6 8.2 %collective-permute-start.82 = (f32[6,1,256]{2,1,0:T(1,128)S(1)}, f32[6,1,256]{2,1,0:T(1,128)S(1)}, u32[]{:S(2)}, u32[]{:S(2)}) collective-permute-start(f32[6,1,256]{2,1,0:T(1,128)S(1)} %get-tuple-element.16), channel_id=1, source_target_pairs={{0,1},{1,2},{2,3},{3,4},{4,5},{5,6},{6,7},{7,8},{8,9},{9,10},{10,1... | collective-permute-start | bytes 18440 | tf_op jit(solution)/shard_map/ppermute | solution.py:19
  471.5 8.2 %collective-permute-start.86 = (f32[6,1,256]{2,1,0:T(1,128)S(1)}, f32[6,1,256]{2,1,0:T(1,128)S(1)}, u32[]{:S(2)}, u32[]{:S(2)}) collective-permute-start(f32[6,1,256]{2,1,0:T(1,128)S(1)} %get-tuple-element.14), channel_id=1, source_target_pairs={{0,1},{1,2},{2,3},{3,4},{4,5},{5,6},{6,7},{7,8},{8,9},{9,10},{10,1... | collective-permute-start | bytes 18440 | tf_op jit(solution)/shard_map/ppermute | solution.py:19
  518.3 8.2 %collective-permute-start.94 = (f32[6,1,256]{2,1,0:T(1,128)S(1)}, f32[6,1,256]{2,1,0:T(1,128)S(1)}, u32[]{:S(2)}, u32[]{:S(2)}) collective-permute-start(f32[6,1,256]{2,1,0:T(1,128)S(1)} %get-tuple-element.12), channel_id=1, source_target_pairs={{0,1},{1,2},{2,3},{3,4},{4,5},{5,6},{6,7},{7,8},{8,9},{9,10},{10,1... | collective-permute-start | bytes 18440 | tf_op jit(solution)/shard_map/ppermute | solution.py:19
  (50 other events, 360.7 us)
where the time goes:
time: 531 us; the launch traced here: 527 us
  starting transfers between devices  320 us (60%)
  waiting for transfers between devices  126 us (24%)
  local copies, waits for them, and re-layouts  48.9 us (9%)
  other arithmetic  30 us (6%)
    ppermute x46, starting transfers between devices, extended(): lax.ppermute(lax.slice_in_dim(block, block.shape[dim] - width, None, axis...  195 us
    ppermute x46, starting transfers between devices, extended(): lax.ppermute(lax.slice_in_dim(block, 0, width, axis=dim), axis, backward)  119 us
    ppermute x46, waiting for transfers between devices, extended(): lax.ppermute(lax.slice_in_dim(block, block.shape[dim] - width, None, axis...  90.1 us
    another operation x4, local copies, waits for them, and re-layouts, shrink(): values.reshape(values.shape[0] // 2, 2, values.shape[1] // 2, 2, values.s...  23 us
    ppermute x3, waiting for transfers between devices, passed_along(): return lax.ppermute(block, axis, route)  22.7 us
    reshape x4, local copies, waits for them, and re-layouts, shrink(): values.reshape(values.shape[0] // 2, 2, values.shape[1] // 2, 2, values.s...  22.2 us
    reduce_sum x8, other arithmetic, shrink(): return values.reshape(values.shape[0] // 2, 2, values.shape[1] // 2, 2, v...  20.3 us
    ppermute x46, waiting for transfers between devices, extended(): lax.ppermute(lax.slice_in_dim(block, 0, width, axis=dim), axis, backward)  13.5 us
  transfers between devices with their start and end apart: 95, of which 35 were waited for; matrix products, arithmetic and copies ran while one was open for 8% of the time, Pallas kernels for 0%

commit v1 on v0

v1 whole, which is shorter than its diff:
```python
import jax
import jax.numpy as jnp
from jax import lax
from jax.experimental import pallas as pl
from jax.experimental.pallas import tpu as pltpu
from jax.sharding import PartitionSpec as P

MESH = pl.DeviceIdType.MESH
SECTIONS = 4
RELAX = 0.8


def chebyshev_coefficients(sections):
    damping = 0.05
    centre_point = 1.0 + damping / (sections * sections)
    chebyshev = [1.0, centre_point]
    slopes = [0.0, 1.0]
    for degree in range(2, sections + 1):
        chebyshev.append(2.0 * centre_point * chebyshev[degree - 1] - chebyshev[degree - 2])
        slopes.append(
            2.0 * chebyshev[degree - 1]
            + 2.0 * centre_point * slopes[degree - 1]
            - slopes[degree - 2]
        )
    slope_ratio = chebyshev[sections] / slopes[sections]
    weights = [1.0 / entry for entry in chebyshev]
    scales = [0.0, 0.0]
    carries = [0.0, 0.0]
    tildes = [0.0, slope_ratio / centre_point]
    for degree in range(2, sections + 1):
        scales.append(2.0 * weights[degree] * centre_point / weights[degree - 1])
        carries.append(-weights[degree] / weights[degree - 2])
        tildes.append(2.0 * weights[degree] * slope_ratio / weights[degree - 1])
    return (scales, carries, tildes)


DIRS = ((1, 0), (-1, 0), (0, 1), (0, -1), (1, 1), (1, -1), (-1, 1), (-1, -1))


def cuts(step, low, count, wide):
    if step == 0:
        return pl.ds(low, count), pl.ds(low, count)
    if step == 1:
        return pl.ds(low + count - wide, wide), pl.ds(low - wide, wide)
    return pl.ds(low, wide), pl.ds(low + count, wide)


def fine_box(d, deep, rows, corner):
    dz, dr = d
    hz, hr = (corner, corner) if dz and dr else (deep, rows)
    z_src, z_dst = cuts(dz, 4, 4, hz)
    every = pl.ds(0, 2)
    if dr == 0:
        box = (pl.ds(0, 4), every, pl.ds(2, 4))
        return (z_src, *box), (z_dst, *box)
    rows_at = pl.ds(4 - hr, hr) if dr == 1 else pl.ds(0, hr)
    s_src, s_dst = (5, 1) if dr == 1 else (2, 6)
    return (
        (z_src, rows_at, every, pl.ds(s_src, 1)),
        (z_dst, rows_at, every, pl.ds(s_dst, 1)),
    )


def coarse_box(d):
    dz, dr = d
    deep, rows = (1, 1) if dz and dr else (2, 2)
    z_src, z_dst = cuts(dz, 2, 2, deep)
    if dr == 0:
        return (z_src, pl.ds(0, 2), pl.ds(2, 4)), (z_dst, pl.ds(0, 2), pl.ds(2, 4))
    rows_at = pl.ds(2 - rows, rows) if dr == 1 else pl.ds(0, rows)
    s_src, s_dst = (5, 1) if dr == 1 else (2, 6)
    return (z_src, rows_at, pl.ds(s_src, 1)), (z_dst, rows_at, pl.ds(s_dst, 1))


def lanes(shape):
    return lax.broadcasted_iota(jnp.int32, shape, len(shape) - 1)


def around(centre, fine):
    axis = centre.ndim - 2
    row_after = jnp.concatenate([centre[1:], pltpu.roll(centre[:1], 7, axis)], 0)
    row_before = jnp.concatenate([pltpu.roll(centre[-1:], 1, axis), centre[:-1]], 0)
    if fine:
        even, odd = centre[:, 0], centre[:, 1]
    else:
        even, odd = centre, centre
    at = lanes(even.shape)
    last = even.ndim - 1
    shifted_up = jnp.where(at == 127, 0.0, pltpu.roll(even, 127, last))
    shifted_down = jnp.where(at == 0, 0.0, pltpu.roll(odd, 1, last))
    if not fine:
        return row_after, row_before, shifted_up, shifted_down
    return (
        row_after,
        row_before,
        jnp.stack([odd, shifted_up], 1),
        jnp.stack([shifted_down, even], 1),
    )


def operator(field, coeffs, z, fine=True):
    centre, after, before = field[z], field[z + 1], field[z - 1]
    ra, rb, ca, cb = around(centre, fine)
    spread = coeffs[0, z] * (after + before + ra + rb + ca + cb - 6.0 * centre)
    drift = coeffs[1, z] * (after - before) + coeffs[2, z] * (ra - rb) + coeffs[3, z] * (ca - cb)
    return centre, spread, drift


def spread_out(value):
    wide = jnp.concatenate([value[:1], value[:1], value[1:], value[1:]], 0)
    return jnp.stack([wide, wide], 1)


def gathered(value, index):
    return jnp.take_along_axis(value, index, axis=1, mode="promise_in_bounds")


def split_columns(rows):
    low, high = rows[:, :128], rows[:, 128:]
    at = lanes(low.shape)
    source = (2 * at) % 128
    first = at < 64
    even = jnp.where(first, gathered(low, source), gathered(high, source))
    odd = jnp.where(first, gathered(low, source + 1), gathered(high, source + 1))
    return even, odd


def join_columns(even, odd):
    at = lanes(even.shape)
    half = at // 2
    is_even = at % 2 == 0
    low = jnp.where(is_even, gathered(even, half), gathered(odd, half))
    high = jnp.where(is_even, gathered(even, half + 64), gathered(odd, half + 64))
    return low, high


def kernel(
    s_ref, d_ref, v_ref, o_ref,
    own, co, sa, sb, ta, ua, weight, fe, bb, v1, v2, e1, e2, cco, cweight,
    fx, sx, xin, xout, res, dealt,
    s_send, s_recv, c_send, c_recv, f_send, f_recv, b_send, b_recv, e_send, e_recv, m_send, m_recv,
):
    tm, slab, coarse = (lax.axis_index(a) for a in ("tm", "slab", "coarse"))
    slabs, coarses = lax.axis_size("slab"), lax.axis_size("coarse")

    def at(dz, dr):
        z, r = slab + dz, coarse + dr
        return z, r, (z >= 0) & (z < slabs) & (r >= 0) & (r < coarses)

    sibling = tm + 1 - 2 * lax.rem(tm, 2)
    barrier = pltpu.get_barrier_semaphore()
    count = jnp.int32(1)
    pl.semaphore_signal(barrier, inc=1, device_id=(sibling, slab, coarse), device_id_type=MESH)
    for dz, dr in DIRS:
        z, r, there = at(dz, dr)

        @pl.when(there)
        def _():
            for t in (tm, sibling):
                pl.semaphore_signal(barrier, inc=1, device_id=(t, z, r), device_id_type=MESH)

        count = count + 2 * there.astype(jnp.int32)
    for a, b in ((1, 2), (1, 3)):
        for me, other in ((a, b), (b, a)):
            here = tm == me

            @pl.when(here)
            def _():
                pl.semaphore_signal(
                    barrier, inc=1, device_id=(other, slab, coarse), device_id_type=MESH
                )

            count = count + here.astype(jnp.int32)

    def arrange(z, _):
        for source, target, scale in (
            (s_ref.at[z], own.at[z], None),
            (d_ref.at[z], co.at[0, z + 4], None),
            (v_ref.at[0, z], co.at[1, z + 4], 0.5),
            (v_ref.at[1, z], co.at[2, z + 4], 0.5),
            (v_ref.at[2, z], co.at[3, z + 4], 0.5),
        ):
            for p, part in enumerate(split_columns(source[...])):
                dealt[z, p] = part if scale is None else scale * part
                for i in range(4):
                    target[i, p, 2:6, :] = dealt[z, p, pl.ds(i, 4, stride=4), :]
        return 0

    lax.fori_loop(0, 4, arrange, 0)
    pl.semaphore_wait(barrier, count)

    def copy(src, dst, send, recv, device):
        return pltpu.make_async_remote_copy(
            src_ref=src, dst_ref=dst, send_sem=send, recv_sem=recv, device_id=device, device_id_type=MESH
        )

    def own_box(z):
        return (pl.ds(z, 4), pl.ds(0, 4), pl.ds(0, 2), pl.ds(2, 4))

    def state_copy(n):
        if n == 8:
            return copy(
                own.at[own_box(0)], sa.at[own_box(4)], s_send.at[8], s_recv.at[8],
                (sibling, slab, coarse),
            )
        z, r, _ = at(*DIRS[n])
        (zs, *src), dst = fine_box(DIRS[n], 4, 4, 3)
        src = (pl.ds(zs.start - 4, zs.size), *src)
        return copy(own.at[src], sa.at[dst], s_send.at[n], s_recv.at[n], (sibling, z, r))

    def coeff_copy(n):
        z, r, _ = at(*DIRS[n])
        src, dst = fine_box(DIRS[n], 3, 3, 2)
        every = pl.ds(0, 4)
        return copy(
            co.at[(every, *src)], co.at[(every, *dst)], c_send.at[n], c_recv.at[n], (tm, z, r)
        )

    def step_copy(n):
        z, r, _ = at(*DIRS[n])
        src, dst = fine_box(DIRS[n], 4, 4, 3)
        return copy(sb.at[src], sb.at[dst], f_send.at[n], f_recv.at[n], (tm, z, r))

    def solve_copy(k):
        def make(n):
            z, r, _ = at(*DIRS[n])
            src, dst = fine_box(DIRS[n], 2, 2, 1)
            return copy(
                bb.at[(k, *src)], bb.at[(k, *dst)], b_send.at[k, n], b_recv.at[k, n], (tm, z, r)
            )

        return make

    def guess_copy(k):
        def make(n):
            z, r, _ = at(*DIRS[n])
            src, dst = coarse_box(DIRS[n])
            return copy(
                e1.at[(k, *src)], e1.at[(k, *dst)], e_send.at[k, n], e_recv.at[k, n], (tm, z, r)
            )

        return make

    def start(make, order=range(8)):
        for n in order:
            _, _, there = at(*DIRS[n])
            pl.when(there)(lambda n=n: make(n).start())

    def arrive(make):
        for n in range(8):
            _, _, there = at(-DIRS[n][0], -DIRS[n][1])
            pl.when(there)(lambda n=n: make(n).wait_recv())

    def sent(make):
        for n in range(8):
            _, _, there = at(*DIRS[n])
            pl.when(there)(lambda n=n: make(n).wait_send())

    far = (4, 5, 6, 7, 2, 3, 0, 1)
    start(state_copy, far)
    state_copy(8).start()
    start(coeff_copy, far)

    here = (slab, coarse)
    window = copy(own.at[own_box(0)], sx.at[own_box(0)], m_send.at[0], m_recv.at[0], (1, *here))
    pl.when(tm == 2)(window.start)

    def outside(edge, layers, sublanes, coarse_layers):
        @pl.when(edge)
        def _():
            z, n = layers
            zero = jnp.zeros((4, 2, sublanes[1], 128), jnp.float32)
            s = pl.ds(*sublanes)

            def clear(q, _):
                for m in range(4):
                    co[m, z + q, :, :, s, :] = zero
                for field in (sa, sb, bb.at[0], bb.at[1], bb.at[2]):
                    field[z + q, :, :, s, :] = zero
                return 0

            lax.fori_loop(0, n, clear, 0)
            for k in range(3):
                for q in range(coarse_layers[0], coarse_layers[0] + coarse_layers[1]):
                    e1[k, q, :, s, :] = jnp.zeros((2, sublanes[1], 128), jnp.float32)

    outside(slab == 0, (0, 4), (0, 8), (0, 2))
    outside(slab == slabs - 1, (8, 4), (0, 8), (4, 2))
    outside(coarse == 0, (0, 12), (1, 1), (0, 6))
    outside(coarse == coarses - 1, (0, 12), (6, 1), (0, 6))

    arrive(state_copy)
    state_copy(8).wait_recv()
    arrive(coeff_copy)

    scales, carries, tildes = chebyshev_coefficients(SECTIONS)

    def loop(low, high, body):
        def wrapped(z, _):
            body(z)
            return 0

        lax.fori_loop(low, high, wrapped, 0, unroll=2)

    def fine_step(begin, finish):
        def first(z):
            centre, spread, drift = operator(begin, co, z)
            ta[z] = centre + tildes[1] * (spread - drift)

        def later(degree, current, before, put):
            def body(z):
                centre, spread, drift = operator(current, co, z)
                put(
                    z,
                    scales[degree] * centre
                    + carries[degree] * before[z]
                    + tildes[degree] * (spread - drift),
                )

            return body

        def put_to(ref):
            def put(z, value):
                ref[z] = value

            return put

        loop(1, 11, first)
        loop(2, 10, later(2, ta, begin, put_to(ua)))
        loop(3, 9, later(3, ua, ta, put_to(ta)))
        loop(4, 8, later(4, ta, ua, finish))

    def to_sb(z, value):
        sb[z, :, :, 2:6, :] = value[:, :, 2:6, :]

    def to_fe(z, value):
        fe[z - 4] = value

    fine_step(sa, to_sb)
    start(step_copy, far)

    def weigh(z):
        weight[z] = RELAX / (1.0 + 12.0 * co[0, z])

    loop(3, 9, weigh)

    def coarse_weigh(q):
        for m in range(4):
            total = co[m, 2 * q] + co[m, 2 * q + 1]
            total = total[:, 0] + total[:, 1]
            total = jnp.concatenate([total[0:1] + total[1:2], total[2:3] + total[3:4]], 0)
            mean = 0.125 * total
            cco[m, q] = mean
            if m == 0:
                cweight[q] = RELAX / (1.0 + 3.0 * mean)

    loop(1, 5, coarse_weigh)
    arrive(step_copy)
    fine_step(sb, to_fe)

    is_lead = lax.rem(tm, 2) == 1
    ends = copy(fe, fx, m_send.at[1], m_recv.at[1], (sibling, *here))
    ends_first = copy(fe, res, m_send.at[1], m_recv.at[1], (sibling, *here))
    crossing = copy(xout, xin, m_send.at[2], m_recv.at[2], (3, *here))
    third = copy(res, res, m_send.at[3], m_recv.at[3], (2, *here))
    pl.when(jnp.logical_not(is_lead))(ends.start)
    pl.when(tm == 1)(ends_first.start)

    def to_bb(k, z, value):
        bb[k, z + 4, :, :, 2:6, :] = value[:, :, 2:6, :]

    @pl.when(tm == 1)
    def _():
        for z in range(4):
            to_bb(0, z, fe[z] - own[z])

    @pl.when(tm == 3)
    def _():
        crossing.wait_recv()
        for z in range(4):
            value = fe[z] + xin[z]
            res[z] = value
            to_bb(2, z, value - own[z])
        third.start()

    def solve(k, _):
        b = bb.at[k]
        start(solve_copy(k), far)
        arrive(solve_copy(k))

        def smooth(z):
            centre, spread, drift = operator(b, co, z)
            v1[z] = centre + (2.0 * weight[z]) * (spread - drift)

        loop(3, 9, smooth)

        def restrict(q):
            total = None
            for z in (2 * q, 2 * q + 1):
                centre, spread, drift = operator(v1, co, z)
                misfit = b[z] - centre + 2.0 * (spread - drift)
                total = misfit if total is None else total + misfit
            total = total[:, 0] + total[:, 1]
            total = jnp.concatenate([total[0:1] + total[1:2], total[2:3] + total[3:4]], 0)
            guess = cweight[q] * (0.125 * total)
            e1[k, q, :, 2:6, :] = guess[:, 2:6, :]

        loop(2, 4, restrict)
        start(guess_copy(k), far)
        arrive(guess_copy(k))

        def correct(q):
            centre, spread, drift = operator(e1.at[k], cco, q, fine=False)
            w = cweight[q]
            second = (2.0 - w) * centre + w * (0.5 * spread - drift)
            wide = spread_out(second)
            for z in (2 * q, 2 * q + 1):
                v2[z] = v1[z] + wide

        loop(1, 5, correct)

        def finish(z):
            centre, spread, drift = operator(v2, co, z)
            xout[z - 4] = centre + weight[z] * (b[z] - centre + 2.0 * (spread - drift))

        loop(4, 8, finish)

        @pl.when(k == 0)
        def _():
            ends.wait_recv()
            window.wait_recv()
            for z in range(4):
                value = fx[z] + xout[z]
                res[z] = value
                to_bb(1, z, value - sx[z])

        @pl.when(k == 1)
        def _():
            crossing.start()

        sent(solve_copy(k))
        sent(guess_copy(k))
        return 0

    low = jnp.where(tm == 1, 0, 2)
    high = jnp.where(tm == 1, 2, jnp.where(tm == 3, 3, 2))
    lax.fori_loop(low, high, solve, 0)

    @pl.when(tm == 3)
    def _():
        ends.wait_recv()
        third.wait_send()
        for z in range(4):
            res[z] = fx[z] + xout[z]

    pl.when(tm == 0)(ends_first.wait_recv)
    pl.when(tm == 2)(third.wait_recv)

    def give(z, _):
        for p in range(2):
            for i in range(4):
                dealt[z, p, pl.ds(i, 4, stride=4), :] = res[z, i, p, 2:6, :]
        low_part, high_part = join_columns(dealt[z, 0], dealt[z, 1])
        o_ref[z, :, 0:128] = low_part
        o_ref[z, :, 128:256] = high_part
        return 0

    lax.fori_loop(0, 4, give, 0)

    sent(state_copy)
    state_copy(8).wait_send()
    sent(coeff_copy)
    sent(step_copy)
    pl.when(tm == 2)(window.wait_send)
    pl.when(jnp.logical_not(is_lead))(ends.wait_send)
    pl.when(tm == 1)(ends_first.wait_send)
    pl.when(tm == 1)(crossing.wait_send)


def per_device(states, diffusivity, velocity):
    def vmem(*shape):
        return pltpu.VMEM(shape + (8, 128), jnp.float32)

    dma = pltpu.SemaphoreType.DMA
    block = pl.BlockSpec(memory_space=pltpu.VMEM)
    out = pl.pallas_call(
        kernel,
        name="parareal",
        out_shape=jax.ShapeDtypeStruct(diffusivity.shape, jnp.float32),
        in_specs=[block] * 3,
        out_specs=block,
        scratch_shapes=[
            vmem(4, 4, 2),
            vmem(4, 12, 4, 2),
            vmem(12, 4, 2),
            vmem(12, 4, 2),
            vmem(12, 4, 2),
            vmem(12, 4, 2),
            vmem(12, 4, 2),
            vmem(4, 4, 2),
            vmem(3, 12, 4, 2),
            vmem(12, 4, 2),
            vmem(12, 4, 2),
            vmem(3, 6, 2),
            vmem(6, 2),
            vmem(4, 6, 2),
            vmem(6, 2),
            vmem(4, 4, 2),
            vmem(4, 4, 2),
            vmem(4, 4, 2),
            vmem(4, 4, 2),
            vmem(4, 4, 2),
            pltpu.VMEM((4, 2, 16, 128), jnp.float32),
            dma((9,)), dma((9,)), dma((8,)), dma((8,)), dma((8,)), dma((8,)),
            dma((3, 8)), dma((3, 8)), dma((3, 8)), dma((3, 8)), dma((4,)), dma((4,)),
        ],
        compiler_params=pltpu.CompilerParams(
            collective_id=0, has_side_effects=True, vmem_limit_bytes=32 * 1024 * 1024
        ),
    )(states[0], diffusivity, velocity)
    return out[None]


def solution(mesh):
    return jax.shard_map(
        per_device,
        mesh=mesh,
        in_specs=(
            P("tm", "slab", "coarse", None),
            P("slab", "coarse", None),
            P(None, "slab", "coarse", None),
        ),
        out_specs=P("tm", "slab", "coarse", None),
        check_vma=False,
    )
```

time: 531 us -> 62.8 us (0.12)
  the two profiles are of different devices: /device:TPU:226 before, /device:TPU:57 now
where the time goes in v1:
time: 62.8 us; the launch traced here: 62.5 us
  Pallas kernels  59.3 us (94%)
  local copies, waits for them, and re-layouts  3.24 us (5%)
    pallas_call x1, Pallas kernels, per_device(): pl.pallas_call(kernel, name='parareal', out_shape=jax.ShapeDtypeStruct(di...  59.3 us
    unnamed x7, local copies, waits for them, and re-layouts  3.24 us

profile of v1, /device:TPU:57, one launch (start us, length us, event | category | flops | bytes accessed | tf_op | source)
XLA Modules:
  0.0 62.5 jit_solution(11131206783661149962)
XLA Ops:
  0.0 0.0 copy-start
  0.0 0.9 %copy-done = f32[3,4,16,256]{3,2,1,0:T(8,128)S(1)} copy-done((f32[3,4,16,256]{3,2,1,0:T(8,128)S(1)}, f32[3,4,16,256]{3,2,1,0:T(8,128)}, u32[]{:S(2)}) %copy-start) | copy-done | bytes 196632
  0.9 0.0 copy-start.1
  0.9 0.8 %copy-done.1 = f32[1,4,16,256]{3,2,1,0:T(8,128)S(1)} copy-done((f32[1,4,16,256]{3,2,1,0:T(8,128)S(1)}, f32[1,4,16,256]{3,2,1,0:T(8,128)}, u32[]{:S(2)}) %copy-start.1) | copy-done | bytes 65560
  1.8 0.0 copy-start.2
  1.8 0.8 %copy-done.2 = f32[4,16,256]{2,1,0:T(8,128)S(1)} copy-done((f32[4,16,256]{2,1,0:T(8,128)S(1)}, f32[4,16,256]{2,1,0:T(8,128)}, u32[]{:S(2)}) %copy-start.2) | copy-done | bytes 65560
  2.6 59.3 %parareal.1 = f32[4,16,256]{2,1,0:T(8,128)S(1)} custom-call(f32[4,16,256]{2,1,0:T(8,128)S(1)} %bitcast.3, f32[4,16,256]{2,1,0:T(8,128)S(1)} %copy-done.2, f32[3,4,16,256]{3,2,1,0:T(8,128)S(1)} %copy-done), custom_call_target="tpu_custom_call" | custom-call | tf_op jit(solution)/shard_map/parareal/pallas_call | solution.py:486
  61.9 0.6 %copy.5 = f32[1,4,16,256]{3,2,1,0:T(8,128)} copy(f32[1,4,16,256]{3,2,1,0:T(8,128)S(1)} %bitcast.2) | data formatting | bytes 131072
Async XLA Ops:
  0.0 0.9 %copy-start = (f32[3,4,16,256]{3,2,1,0:T(8,128)S(1)}, f32[3,4,16,256]{3,2,1,0:T(8,128)}, u32[]{:S(2)}) copy-start(f32[3,4,16,256]{3,2,1,0:T(8,128)} %v_ref.1) | copy-start | bytes 589828
  0.9 0.8 %copy-start.1 = (f32[1,4,16,256]{3,2,1,0:T(8,128)S(1)}, f32[1,4,16,256]{3,2,1,0:T(8,128)}, u32[]{:S(2)}) copy-start(f32[1,4,16,256]{3,2,1,0:T(8,128)} %param.3) | copy-start | bytes 196612
  1.8 0.8 %copy-start.2 = (f32[4,16,256]{2,1,0:T(8,128)S(1)}, f32[4,16,256]{2,1,0:T(8,128)}, u32[]{:S(2)}) copy-start(f32[4,16,256]{2,1,0:T(8,128)} %d_ref.1) | copy-start | bytes 196612

commit v2 on v1

v2 whole, which is shorter than its diff:
```python
import jax
import jax.numpy as jnp
from jax import lax
from jax.experimental import pallas as pl
from jax.experimental.pallas import tpu as pltpu
from jax.sharding import PartitionSpec as P

MESH = pl.DeviceIdType.MESH
SECTIONS = 4
RELAX = 0.8


def chebyshev_coefficients(sections):
    damping = 0.05
    centre_point = 1.0 + damping / (sections * sections)
    chebyshev = [1.0, centre_point]
    slopes = [0.0, 1.0]
    for degree in range(2, sections + 1):
        chebyshev.append(2.0 * centre_point * chebyshev[degree - 1] - chebyshev[degree - 2])
        slopes.append(
            2.0 * chebyshev[degree - 1]
            + 2.0 * centre_point * slopes[degree - 1]
            - slopes[degree - 2]
        )
    slope_ratio = chebyshev[sections] / slopes[sections]
    weights = [1.0 / entry for entry in chebyshev]
    scales = [0.0, 0.0]
    carries = [0.0, 0.0]
    tildes = [0.0, slope_ratio / centre_point]
    for degree in range(2, sections + 1):
        scales.append(2.0 * weights[degree] * centre_point / weights[degree - 1])
        carries.append(-weights[degree] / weights[degree - 2])
        tildes.append(2.0 * weights[degree] * slope_ratio / weights[degree - 1])
    return (scales, carries, tildes)


DIRS = ((1, 0), (-1, 0), (0, 1), (0, -1), (1, 1), (1, -1), (-1, 1), (-1, -1))


def cuts(step, low, count, wide):
    if step == 0:
        return pl.ds(low, count), pl.ds(low, count)
    if step == 1:
        return pl.ds(low + count - wide, wide), pl.ds(low - wide, wide)
    return pl.ds(low, wide), pl.ds(low + count, wide)


def fine_box(d, deep, rows, corner, blocks=1):
    dz, dr = d
    hz, hr = corner if dz and dr else (deep, rows)
    z_src, z_dst = cuts(dz, 4, 4, hz)
    every = pl.ds(0, 2)
    if dr == 0:
        box = (pl.ds(0, 4), every, pl.ds(2, 4))
        return (z_src, *box), (z_dst, *box)
    rows_at = pl.ds(4 - hr, hr) if dr == 1 else pl.ds(0, hr)
    s_src, s_dst = (6 - blocks, 2 - blocks) if dr == 1 else (2, 6)
    return (
        (z_src, rows_at, every, pl.ds(s_src, blocks)),
        (z_dst, rows_at, every, pl.ds(s_dst, blocks)),
    )


def coarse_box(d, blocks):
    dz, dr = d
    z_src, z_dst = cuts(dz, 2, 2, 2)
    every = pl.ds(0, 2)
    if dr == 0:
        return (z_src, every, pl.ds(2, 4)), (z_dst, every, pl.ds(2, 4))
    blocks = 1 if dz else blocks
    s_src, s_dst = (6 - blocks, 2 - blocks) if dr == 1 else (2, 6)
    return (z_src, every, pl.ds(s_src, blocks)), (z_dst, every, pl.ds(s_dst, blocks))


def lanes(shape):
    return lax.broadcasted_iota(jnp.int32, shape, len(shape) - 1)


def around(centre, fine):
    axis = centre.ndim - 2
    row_after = jnp.concatenate([centre[1:], pltpu.roll(centre[:1], 7, axis)], 0)
    row_before = jnp.concatenate([pltpu.roll(centre[-1:], 1, axis), centre[:-1]], 0)
    if fine:
        even, odd = centre[:, 0], centre[:, 1]
    else:
        even, odd = centre, centre
    at = lanes(even.shape)
    last = even.ndim - 1
    shifted_up = jnp.where(at == 127, 0.0, pltpu.roll(even, 127, last))
    shifted_down = jnp.where(at == 0, 0.0, pltpu.roll(odd, 1, last))
    if not fine:
        return row_after, row_before, shifted_up, shifted_down
    return (
        row_after,
        row_before,
        jnp.stack([odd, shifted_up], 1),
        jnp.stack([shifted_down, even], 1),
    )


def operator(field, coeffs, z, fine=True):
    centre, after, before = field[z], field[z + 1], field[z - 1]
    ra, rb, ca, cb = around(centre, fine)
    spread = coeffs[0, z] * (after + before + ra + rb + ca + cb - 6.0 * centre)
    drift = coeffs[1, z] * (after - before) + coeffs[2, z] * (ra - rb) + coeffs[3, z] * (ca - cb)
    return centre, spread, drift


def spread_out(value):
    wide = jnp.concatenate([value[:1], value[:1], value[1:], value[1:]], 0)
    return jnp.stack([wide, wide], 1)


def gathered(value, index):
    return jnp.take_along_axis(value, index, axis=1, mode="promise_in_bounds")


def split_columns(rows):
    low, high = rows[:, :128], rows[:, 128:]
    at = lanes(low.shape)
    source = (2 * at) % 128
    first = at < 64
    even = jnp.where(first, gathered(low, source), gathered(high, source))
    odd = jnp.where(first, gathered(low, source + 1), gathered(high, source + 1))
    return even, odd


def join_columns(even, odd):
    at = lanes(even.shape)
    half = at // 2
    is_even = at % 2 == 0
    low = jnp.where(is_even, gathered(even, half), gathered(odd, half))
    high = jnp.where(is_even, gathered(even, half + 64), gathered(odd, half + 64))
    return low, high


def kernel(
    s_hbm, d_hbm, v_hbm, o_ref,
    s_ref, d_ref, v_ref,
    own, co, cw, sa, sb, ta, ua, weight, fe, jo, jj, bb, v1, v2, vr, e1, cco, cweight,
    fx, sx, xout, res, dealt,
    in_sem, s_send, s_recv, c_send, c_recv, w_send, w_recv, g_send, g_recv,
    f_send, f_recv, b_send, b_recv, e_send, e_recv, r_send, r_recv, x_send, x_recv,
    m_send, m_recv,
):
    tm, slab, coarse = (lax.axis_index(a) for a in ("tm", "slab", "coarse"))
    slabs, coarses = lax.axis_size("slab"), lax.axis_size("coarse")
    loads = [
        pltpu.make_async_copy(src, dst, in_sem.at[n])
        for n, (src, dst) in enumerate(((s_hbm, s_ref), (d_hbm, d_ref), (v_hbm, v_ref)))
    ]
    for load in loads:
        load.start()

    def at(dz, dr):
        z, r = slab + dz, coarse + dr
        return z, r, (z >= 0) & (z < slabs) & (r >= 0) & (r < coarses)

    core = lax.rem(tm, 2)
    is_lead = core == 1
    sibling = tm + 1 - 2 * core
    across = lax.rem(tm + 2, 4)
    here = (slab, coarse)

    barrier = pltpu.get_barrier_semaphore()
    count = jnp.int32(2)
    for dz, dr in DIRS:
        z, r, there = at(dz, dr)

        @pl.when(there)
        def _():
            for t in (tm, sibling):
                pl.semaphore_signal(barrier, inc=1, device_id=(t, z, r), device_id_type=MESH)

        count = count + 2 * there.astype(jnp.int32)
    for t in (across, sibling):
        pl.semaphore_signal(barrier, inc=1, device_id=(t, *here), device_id_type=MESH)

    def arrange(z, _):
        for source, target, scale in (
            (s_ref.at[z], own.at[z], None),
            (d_ref.at[z], co.at[0, z + 4], None),
            (v_ref.at[0, z], co.at[1, z + 4], 0.5),
            (v_ref.at[1, z], co.at[2, z + 4], 0.5),
            (v_ref.at[2, z], co.at[3, z + 4], 0.5),
        ):
            for p, part in enumerate(split_columns(source[...])):
                dealt[z, p] = part if scale is None else scale * part
                for i in range(4):
                    target[i, p, 2:6, :] = dealt[z, p, pl.ds(i, 4, stride=4), :]
        return 0

    for load in loads:
        load.wait()
    lax.fori_loop(0, 4, arrange, 0)
    pl.semaphore_wait(barrier, count)

    def copy(src, dst, send, recv, device):
        return pltpu.make_async_remote_copy(
            src_ref=src, dst_ref=dst, send_sem=send, recv_sem=recv, device_id=device, device_id_type=MESH
        )

    def own_box(z):
        return (pl.ds(z, 4), pl.ds(0, 4), pl.ds(0, 2), pl.ds(2, 4))

    every = pl.ds(0, 4)
    both = pl.ds(0, 2)

    def state_copy(n):
        z, r, _ = at(*DIRS[n])
        (zs, *src), dst = fine_box(DIRS[n], 4, 4, (3, 3))
        src = (pl.ds(zs.start - 4, zs.size), *src)
        return copy(own.at[src], sa.at[dst], s_send.at[n], s_recv.at[n], (sibling, z, r))

    swap = copy(
        own.at[own_box(0)], sa.at[own_box(4)], s_send.at[8], s_recv.at[8], (sibling, *here)
    )

    def coeff_copy(n):
        z, r, _ = at(*DIRS[n])
        src, dst = fine_box(DIRS[n], 3, 3, (2, 2))
        return copy(
            co.at[(every, *src)], co.at[(every, *dst)], c_send.at[n], c_recv.at[n], (tm, z, r)
        )

    def coeff_pass(n):
        box = (every, *fine_box(DIRS[n], 3, 3, (2, 2))[1])
        return copy(co.at[box], co.at[box], w_send.at[n], w_recv.at[n], (sibling, *here))

    more = []
    for n, (dz, dr) in enumerate(DIRS):
        if dr == 0:
            continue
        z_src, z_dst = cuts(dz, 4, 4, 1 if dz else 4)
        near, away = ((5, 1), (4, 0)) if dr == 1 else ((2, 6), (3, 7))
        more.append((n, (z_src, every, both, pl.ds(away[0], 1)), (z_dst, every, both, pl.ds(away[1], 1))))
        if dz:
            part = pl.ds(0, 2) if dr == 1 else pl.ds(2, 2)
            more.append((n, (z_src, part, both, pl.ds(near[0], 1)), (z_dst, part, both, pl.ds(near[1], 1))))
        else:
            part = pl.ds(0, 1) if dr == 1 else pl.ds(3, 1)
            more.append((n, (z_src, part, both, pl.ds(near[0], 1)), (z_dst, part, both, pl.ds(near[1], 1))))
    more_dirs = [DIRS[n] for n, _, _ in more]

    def more_copy(q):
        n, src, dst = more[q]
        z, r, _ = at(*DIRS[n])
        return copy(
            co.at[(every, *src)], cw.at[(every, *dst)], g_send.at[q], g_recv.at[q], (tm, z, r)
        )

    def step_copy(n):
        z, r, _ = at(*DIRS[n])
        src, dst = fine_box(DIRS[n], 4, 4, (3, 3))
        return copy(sb.at[src], sb.at[dst], f_send.at[n], f_recv.at[n], (tm, z, r))

    def first_copy(n):
        z, r, _ = at(*DIRS[n])
        src, dst = fine_box(DIRS[n], 2, 4, (2, 4), blocks=2)
        return copy(bb.at[(0, *src)], bb.at[(0, *dst)], b_send.at[n], b_recv.at[n], (tm, z, r))

    def layer_copy(k):
        def make(n):
            z, r, _ = at(*DIRS[n])
            z_src, z_dst = cuts(DIRS[n][0], 4, 4, 2)
            box = (every, both, pl.ds(1, 6))
            sem = 8 * k + n
            return copy(
                bb.at[(k, z_src, *box)], bb.at[(k, z_dst, *box)], b_send.at[sem], b_recv.at[sem],
                (tm, z, r),
            )

        return make

    def flat_guess_copy(n):
        z, r, _ = at(*DIRS[n])
        z_src, z_dst = cuts(DIRS[n][0], 2, 2, 2)
        return copy(e1.at[0, z_src], e1.at[0, z_dst], e_send.at[n], e_recv.at[n], (tm, z, r))

    def guess_copy(n):
        z, r, _ = at(*DIRS[n])
        src, dst = coarse_box(DIRS[n], 2)
        return copy(
            e1.at[(1, *src)], e1.at[(1, *dst)], e_send.at[8 + n], e_recv.at[8 + n], (tm, z, r)
        )

    def last_guess_copy(n):
        if n == 8:
            box = (2, pl.ds(2, 2), both, pl.ds(2, 4))
            return copy(e1.at[box], e1.at[box], e_send.at[24], e_recv.at[24], (across, *here))
        z, r, _ = at(*DIRS[n])
        src, dst = coarse_box(DIRS[n], 1)
        return copy(
            e1.at[(2, *src)], e1.at[(2, *dst)], e_send.at[16 + n], e_recv.at[16 + n], (across, z, r)
        )

    def smooth_copy(n):
        z, r, _ = at(*DIRS[n])
        s_src, s_dst = (5, 1) if DIRS[n][1] == 1 else (2, 6)
        box = (pl.ds(3, 6), pl.ds(1, 2), both)
        return copy(
            v1.at[(*box, pl.ds(s_src, 1))], vr.at[(*box, pl.ds(s_dst, 1))],
            r_send.at[n], r_recv.at[n], (tm, z, r),
        )

    def jump_copy(field, n):
        z, r, _ = at(*DIRS[n])
        src, dst = fine_box(DIRS[n], 4, 2, (1, 1))
        return lambda target: copy(
            field.at[src], jj.at[(target, *dst)], r_send.at[n - 2], r_recv.at[n - 2 + 4 * target],
            ((sibling, z, r) if target == 0 else (tm, z, r)),
        )

    def start(make, order=range(8), dirs=DIRS):
        for n in order:
            _, _, there = at(*dirs[n])
            pl.when(there)(lambda n=n: make(n).start())

    def arrive(make, order=range(8), dirs=DIRS):
        for n in order:
            _, _, there = at(-dirs[n][0], -dirs[n][1])
            pl.when(there)(lambda n=n: make(n).wait_recv())

    def sent(make, order=range(8), dirs=DIRS):
        for n in order:
            _, _, there = at(*dirs[n])
            pl.when(there)(lambda n=n: make(n).wait_send())

    far = (4, 5, 6, 7, 2, 3, 0, 1)
    heavy = (0, 1, 4, 5, 6, 7, 2, 3)
    along = (0, 1)
    beside = (2, 3)
    pl.when(is_lead)(lambda: start(coeff_copy, heavy))
    start(state_copy, heavy)
    swap.start()

    window = copy(own, sx, m_send.at[0], m_recv.at[0], (across, *here))
    pl.when(tm == 2)(window.start)

    def zero(n):
        return jnp.zeros((4, 2, n, 128), jnp.float32)

    def loop(low, high, body, unroll=2):
        def wrapped(z, _):
            body(z)
            return 0

        lax.fori_loop(low, high, wrapped, 0, unroll=unroll)

    for edge, begin, begin_coarse in ((slab == 0, 0, 0), (slab == slabs - 1, 8, 4)):

        @pl.when(edge)
        def _():
            def clear(z):
                for m in range(4):
                    co[m, z] = zero(8)
                    cw[m, z] = zero(8)
                for field in (sa, sb, bb.at[0], bb.at[1], bb.at[2]):
                    field[z] = zero(8)

            loop(begin, begin + 4, clear)
            for k in range(3):
                for z in range(begin_coarse, begin_coarse + 2):
                    e1[k, z] = jnp.zeros((2, 8, 128), jnp.float32)

    for edge, begin in ((coarse == 0, 0), (coarse == coarses - 1, 6)):

        @pl.when(edge)
        def _():
            s = pl.ds(begin, 2)

            def clear(z):
                for m in range(4):
                    co[m, z, :, :, s, :] = zero(2)
                    cw[m, z, :, :, s, :] = zero(2)
                for field in (sa, sb, bb.at[0], vr):
                    field[z, :, :, s, :] = zero(2)

            loop(0, 12, clear)
            for k in range(2):

                @pl.when(tm == 1 + 2 * k)
                def _():
                    for z in range(4, 8):
                        jj[k, z, :, :, s, :] = zero(2)

            for k in (1, 2):
                for z in range(6):
                    e1[k, z, :, s, :] = jnp.zeros((2, 2, 128), jnp.float32)

    arrive(state_copy)
    swap.wait_recv()
    pl.when(is_lead)(lambda: arrive(coeff_copy))
    pl.when(jnp.logical_not(is_lead))(lambda: arrive(coeff_pass))

    scales, carries, tildes = chebyshev_coefficients(SECTIONS)

    def fine_step(begin, finish):
        def first(z):
            centre, spread, drift = operator(begin, co, z)
            ta[z] = centre + tildes[1] * (spread - drift)

        def later(degree, current, before, put):
            def body(z):
                centre, spread, drift = operator(current, co, z)
                put(
                    z,
                    scales[degree] * centre
                    + carries[degree] * before[z]
                    + tildes[degree] * (spread - drift),
                )

            return body

        def put_to(ref):
            def put(z, value):
                ref[z] = value

            return put

        loop(1, 11, first)
        loop(2, 10, later(2, ta, begin, put_to(ua)))
        loop(3, 9, later(3, ua, ta, put_to(ta)))
        loop(4, 8, later(4, ta, ua, finish))

    def to_own_rows(target, z, value):
        target[z, :, :, 2:6, :] = value[:, :, 2:6, :]

    def to_fe(z, value):
        fe[z - 4] = value

    fine_step(sa, lambda z, value: to_own_rows(sb, z, value))
    start(step_copy, far)

    @pl.when(is_lead)
    def _():
        for n in range(8):
            _, _, there = at(-DIRS[n][0], -DIRS[n][1])
            pl.when(there)(lambda n=n: coeff_pass(n).start())

    pl.when(tm == 1)(lambda: start(more_copy, range(len(more)), more_dirs))

    arrive(step_copy)
    fine_step(sb, to_fe)

    def weigh(z):
        weight[z] = RELAX / (1.0 + 12.0 * co[0, z])

    def halves(value):
        value = value[:, 0] + value[:, 1]
        return 0.125 * jnp.concatenate([value[0:1] + value[1:2], value[2:3] + value[3:4]], 0)

    def coarse_weigh(q):
        for m in range(4):
            mean = halves(co[m, 2 * q] + co[m, 2 * q + 1])
            cco[m, q] = mean
            if m == 0:
                cweight[q] = RELAX / (1.0 + 3.0 * mean)

    def merge(low, high, first, last):
        def body(z):
            for m in range(4):
                for part, sub in ((every, 0), (every, 7), (first, 1), (last, 6)):
                    at_rows = (m, z, part, slice(None), pl.ds(sub, 1), slice(None))
                    co[at_rows] = cw[at_rows]

        for z in range(low, high):
            body(z)

    def weights():
        loop(3, 9, weigh)
        loop(1, 5, coarse_weigh)

    ends = copy(fe, fx, m_send.at[1], m_recv.at[1], (sibling, *here))
    ends_first = copy(fe, res, m_send.at[1], m_recv.at[1], (sibling, *here))
    jump = copy(
        jo.at[own_box(4)], jj.at[(0, *own_box(4))], m_send.at[2], m_recv.at[2], (sibling, *here)
    )
    jump_box = (1, pl.ds(4, 4), every, both, pl.ds(1, 6))
    last_jump = copy(jj.at[jump_box], jj.at[jump_box], m_send.at[4], m_recv.at[4], (across, *here))
    third = copy(res, res, m_send.at[3], m_recv.at[3], (sibling, *here))
    cross_boxes = [(2, pl.ds(low, n), every, both, pl.ds(1, 6)) for low, n in ((4, 4), (2, 2), (8, 2))]

    def cross(n):
        box = cross_boxes[n]
        return copy(bb.at[box], bb.at[box], x_send.at[n], x_recv.at[n], (across, *here))

    @pl.when(tm == 0)
    def _():
        window.wait_recv()
        for z in range(4):
            jo[z + 4] = fe[z] - sx[z]
        start(lambda n: jump_copy(jo, n)(0), beside)
        jump.start()
        ends.start()
        ends_first.wait_recv()

    @pl.when(tm == 2)
    def _():
        ends.start()
        third.wait_recv()

    def solve_smooth(b):
        def smooth(z):
            centre, spread, drift = operator(b, co, z)
            v1[z] = centre + (2.0 * weight[z]) * (spread - drift)

        loop(3, 9, smooth)

    def solve_restrict(b, put):
        def restrict(q):
            total = None
            for z in (2 * q, 2 * q + 1):
                centre, spread, drift = operator(v1, co, z)
                misfit = b[z] - centre + 2.0 * (spread - drift)
                total = misfit if total is None else total + misfit
            put(q, cweight[q] * halves(total))

        loop(2, 4, restrict)

    def solve_correct(e, base):
        def correct(q):
            centre, spread, drift = operator(e, cco, q, fine=False)
            w = cweight[q]
            wide = spread_out((2.0 - w) * centre + w * (0.5 * spread - drift))
            for z in (2 * q, 2 * q + 1):
                v2[z] = base(z) + wide

        loop(1, 5, correct)

    def solve_finish(b, put):
        def finish(z):
            centre, spread, drift = operator(v2, co, z)
            put(z, centre + weight[z] * (b[z] - centre + 2.0 * (spread - drift)))

        loop(4, 8, finish)

    def put_guess(k):
        def put(q, value):
            e1[k, q, :, 2:6, :] = value[:, 2:6, :]

        return put

    @pl.when(tm == 1)
    def _():
        b = bb.at[0]
        for z in range(4):
            b[z + 4, :, :, 2:6, :] = (fe[z] - own[z])[:, :, 2:6, :]
        start(first_copy, far)
        ends_first.start()
        arrive(more_copy, range(len(more)), more_dirs)
        merge(4, 8, pl.ds(0, 1), pl.ds(3, 1))
        for z in (3, 8):
            merge(z, z + 1, pl.ds(0, 2), pl.ds(2, 2))
        weights()
        arrive(first_copy)
        solve_smooth(b)

        def put_flat(q, value):
            e1[0, q] = value

        solve_restrict(b, put_flat)
        start(flat_guess_copy, along)
        arrive(flat_guess_copy, along)
        solve_correct(e1.at[0], lambda z: v1[z])
        arrive(lambda n: jump_copy(jo, n)(0), beside)
        jump.wait_recv()
        b = bb.at[1]

        def put_first(z, value):
            bb[1, z] = value + jj[0, z]
            xout[z - 4] = value

        solve_finish(bb.at[0], put_first)
        start(layer_copy(1), along)
        ends.wait_recv()
        for z in range(4):
            res[z] = fx[z] + xout[z]

        arrive(layer_copy(1), along)
        solve_smooth(b)
        start(smooth_copy, beside)
        solve_restrict(b, put_guess(1))
        start(guess_copy, far)
        shape = (4, 2, 8, 128)
        i = lax.broadcasted_iota(jnp.int32, shape, 0)
        sub = lax.broadcasted_iota(jnp.int32, shape, 2)
        given = ((sub == 1) | (sub == 6)) & ((i == 1) | (i == 2))
        arrive(smooth_copy, beside)
        arrive(guess_copy)
        solve_correct(e1.at[1], lambda z: jnp.where(given, vr[z], v1[z]))
        last_jump.wait_recv()

        def put_second(z, value):
            bb[2, z] = value + jj[1, z]

        solve_finish(b, put_second)

        b = bb.at[2]
        start(layer_copy(2), along)
        cross(0).start()
        arrive(layer_copy(2), along)
        sent(smooth_copy, beside)
        solve_smooth(b)
        solve_restrict(b, put_guess(2))
        start(last_guess_copy, far)
        last_guess_copy(8).start()
        cross(1).start()
        cross(2).start()

    @pl.when(tm == 3)
    def _():
        for z in range(4):
            value = fe[z] - own[z]
            jo[z + 4] = value
            to_own_rows(jj.at[1], z + 4, value)
        start(lambda n: jump_copy(jo, n)(1), beside)
        weights()
        arrive(lambda n: jump_copy(jo, n)(1), beside)
        last_jump.start()
        b = bb.at[2]
        cross(0).wait_recv()
        for z in range(4):
            res[z] = b[z + 4] + own[z]
        third.start()
        cross(1).wait_recv()
        cross(2).wait_recv()
        solve_smooth(b)
        arrive(last_guess_copy)
        last_guess_copy(8).wait_recv()
        solve_correct(e1.at[2], lambda z: v1[z])
        ends.wait_recv()
        third.wait_send()

        def put_last(z, value):
            res[z - 4] = fx[z - 4] + value

        solve_finish(b, put_last)

    def give(z, _):
        for p in range(2):
            for i in range(4):
                dealt[z, p, pl.ds(i, 4, stride=4), :] = res[z, i, p, 2:6, :]
        low_part, high_part = join_columns(dealt[z, 0], dealt[z, 1])
        o_ref[z, :, 0:128] = low_part
        o_ref[z, :, 128:256] = high_part
        return 0

    lax.fori_loop(0, 4, give, 0)

    sent(state_copy)
    swap.wait_send()
    sent(step_copy)

    @pl.when(is_lead)
    def _():
        sent(coeff_copy)
        for n in range(8):
            _, _, there = at(-DIRS[n][0], -DIRS[n][1])
            pl.when(there)(lambda n=n: coeff_pass(n).wait_send())

    @pl.when(tm == 0)
    def _():
        sent(lambda n: jump_copy(jo, n)(0), beside)
        jump.wait_send()
        ends.wait_send()

    @pl.when(tm == 2)
    def _():
        window.wait_send()
        ends.wait_send()

    @pl.when(tm == 1)
    def _():
        sent(more_copy, range(len(more)), more_dirs)
        sent(first_copy)
        ends_first.wait_send()
        sent(flat_guess_copy, along)
        sent(layer_copy(1), along)
        sent(guess_copy)
        sent(layer_copy(2), along)
        sent(last_guess_copy)
        last_guess_copy(8).wait_send()
        for n in range(3):
            cross(n).wait_send()

    @pl.when(tm == 3)
    def _():
        sent(lambda n: jump_copy(jo, n)(1), beside)
        last_jump.wait_send()


def per_device(states, diffusivity, velocity):
    def vmem(*shape):
        return pltpu.VMEM(shape + (8, 128), jnp.float32)

    dma = pltpu.SemaphoreType.DMA
    block = pl.BlockSpec(memory_space=pl.ANY)
    raw = (states[0], diffusivity, velocity)
    counts = (9, 8, 8, 12, 8, 24, 25, 8, 3, 5)
    out = pl.pallas_call(
        kernel,
        name="parareal",
        out_shape=jax.ShapeDtypeStruct(diffusivity.shape, jnp.float32),
        in_specs=[block] * 3,
        out_specs=pl.BlockSpec(memory_space=pltpu.VMEM),
        scratch_shapes=[pltpu.VMEM(array.shape, jnp.float32) for array in raw]
        + [
            vmem(4, 4, 2),
            vmem(4, 12, 4, 2),
            vmem(4, 12, 4, 2),
            vmem(12, 4, 2),
            vmem(12, 4, 2),
            vmem(12, 4, 2),
            vmem(12, 4, 2),
            vmem(12, 4, 2),
            vmem(4, 4, 2),
            vmem(12, 4, 2),
            vmem(2, 12, 4, 2),
            vmem(3, 12, 4, 2),
            vmem(12, 4, 2),
            vmem(12, 4, 2),
            vmem(12, 4, 2),
            vmem(3, 6, 2),
            vmem(4, 6, 2),
            vmem(6, 2),
            vmem(4, 4, 2),
            vmem(4, 4, 2),
            vmem(4, 4, 2),
            vmem(4, 4, 2),
            pltpu.VMEM((4, 2, 16, 128), jnp.float32),
            dma((3,)),
        ]
        + [dma((n,)) for n in counts for _ in range(2)],
        compiler_params=pltpu.CompilerParams(
            collective_id=0, has_side_effects=True, vmem_limit_bytes=56 * 1024 * 1024
        ),
    )(*raw)
    return out[None]


def solution(mesh):
    return jax.shard_map(
        per_device,
        mesh=mesh,
        in_specs=(
            P("tm", "slab", "coarse", None),
            P("slab", "coarse", None),
            P(None, "slab", "coarse", None),
        ),
        out_specs=P("tm", "slab", "coarse", None),
        check_vma=False,
    )
```

time: 62.8 us -> 52.1 us (0.83)
  Pallas kernels: 59.3 us -> 50.3 us
  local copies, waits for them, and re-layouts: 3.24 us -> 1.47 us
    pallas_call x1, Pallas kernels: 59.3 us -> 50.3 us  [per_device(): pl.pallas_call(kernel, name='parareal', out_shape=jax.ShapeDtypeStruct(di...]
    unnamed x7 -> x1, local copies, waits for them, and re-layouts: 3.24 us -> 1.47 us
where the time goes in v2:
time: 52.1 us; the launch traced here: 51.8 us
  Pallas kernels  50.3 us (97%)
  local copies, waits for them, and re-layouts  1.47 us (3%)
    pallas_call x1, Pallas kernels, per_device(): pl.pallas_call(kernel, name='parareal', out_shape=jax.ShapeDtypeStruct(di...  50.3 us
    unnamed x1, local copies, waits for them, and re-layouts  1.47 us

profile of v2, /device:TPU:57, one launch (start us, length us, event | category | flops | bytes accessed | tf_op | source)
XLA Modules:
  0.0 51.8 jit_solution(8670566858853473989)
XLA Ops:
  0.0 50.3 %parareal.1 = f32[4,16,256]{2,1,0:T(8,128)} custom-call(f32[4,16,256]{2,1,0:T(8,128)} %bitcast.3, f32[4,16,256]{2,1,0:T(8,128)} %d_hbm.1, f32[3,4,16,256]{3,2,1,0:T(8,128)} %v_hbm.1), custom_call_target="tpu_custom_call" | custom-call | tf_op jit(solution)/shard_map/parareal/pallas_call | solution.py:701
  50.3 1.5 %copy.5 = f32[1,4,16,256]{3,2,1,0:T(8,128)} copy(f32[1,4,16,256]{3,2,1,0:T(8,128)} %bitcast.2) | data formatting | bytes 131072

commit v3 on v2

--- a/solution.py
+++ b/solution.py
@@ -340,7 +340,7 @@
     def zero(n):
         return jnp.zeros((4, 2, n, 128), jnp.float32)
 
-    def loop(low, high, body, unroll=2):
+    def loop(low, high, body, unroll=True):
         def wrapped(z, _):
             body(z)
             return 0

time: 52.1 us -> 49.8 us (0.956)
  Pallas kernels: 50.3 us -> 47.9 us
    pallas_call x1, Pallas kernels: 50.3 us -> 47.9 us  [per_device(): pl.pallas_call(kernel, name='parareal', out_shape=jax.ShapeDtypeStruct(di...]
where the time goes in v3:
time: 49.8 us; the launch traced here: 49.4 us
  Pallas kernels  47.9 us (96%)
  local copies, waits for them, and re-layouts  1.47 us (3%)
    pallas_call x1, Pallas kernels, per_device(): pl.pallas_call(kernel, name='parareal', out_shape=jax.ShapeDtypeStruct(di...  47.9 us
    unnamed x1, local copies, waits for them, and re-layouts  1.47 us

profile of v3, /device:TPU:57, one launch (start us, length us, event | category | flops | bytes accessed | tf_op | source)
XLA Modules:
  0.0 49.4 jit_solution(17657523161336013880)
XLA Ops:
  0.0 47.9 %parareal.1 = f32[4,16,256]{2,1,0:T(8,128)} custom-call(f32[4,16,256]{2,1,0:T(8,128)} %bitcast.3, f32[4,16,256]{2,1,0:T(8,128)} %d_hbm.1, f32[3,4,16,256]{3,2,1,0:T(8,128)} %v_hbm.1), custom_call_target="tpu_custom_call" | custom-call | tf_op jit(solution)/shard_map/parareal/pallas_call | solution.py:701
  48.0 1.5 %copy.5 = f32[1,4,16,256]{3,2,1,0:T(8,128)} copy(f32[1,4,16,256]{3,2,1,0:T(8,128)} %bitcast.2) | data formatting | bytes 131072

commit v4 on v3

--- a/solution.py
+++ b/solution.py
@@ -176,23 +176,23 @@
     for t in (across, sibling):
         pl.semaphore_signal(barrier, inc=1, device_id=(t, *here), device_id_type=MESH)
 
-    def arrange(z, _):
-        for source, target, scale in (
-            (s_ref.at[z], own.at[z], None),
-            (d_ref.at[z], co.at[0, z + 4], None),
-            (v_ref.at[0, z], co.at[1, z + 4], 0.5),
-            (v_ref.at[1, z], co.at[2, z + 4], 0.5),
-            (v_ref.at[2, z], co.at[3, z + 4], 0.5),
-        ):
-            for p, part in enumerate(split_columns(source[...])):
-                dealt[z, p] = part if scale is None else scale * part
+    def arrange(m):
+        if m < 3:
+            loads[m].wait()
+        for z in range(4):
+            source = (s_ref, d_ref, v_ref.at[0], v_ref.at[1], v_ref.at[2])[m]
+            target = own.at[z] if m == 0 else co.at[m - 1, z + 4]
+            for p, part in enumerate(split_columns(source[z])):
+                dealt[m, z, p] = 0.5 * part if m > 1 else part
                 for i in range(4):
-                    target[i, p, 2:6, :] = dealt[z, p, pl.ds(i, 4, stride=4), :]
-        return 0
-
-    for load in loads:
-        load.wait()
-    lax.fori_loop(0, 4, arrange, 0)
+                    target[i, p, 2:6, :] = dealt[m, z, p, pl.ds(i, 4, stride=4), :]
+
+    def arrange_coeffs():
+        for m in range(1, 5):
+            arrange(m)
+
+    pl.when(is_lead)(arrange_coeffs)
+    pl.when(jnp.logical_not(is_lead))(lambda: arrange(0))
     pl.semaphore_wait(barrier, count)
 
     def copy(src, dst, send, recv, device):
@@ -330,9 +330,15 @@
     heavy = (0, 1, 4, 5, 6, 7, 2, 3)
     along = (0, 1)
     beside = (2, 3)
-    pl.when(is_lead)(lambda: start(coeff_copy, heavy))
+
+    @pl.when(is_lead)
+    def _():
+        start(coeff_copy, heavy)
+        arrange(0)
+
     start(state_copy, heavy)
     swap.start()
+    pl.when(jnp.logical_not(is_lead))(arrange_coeffs)
 
     window = copy(own, sx, m_send.at[0], m_recv.at[0], (across, *here))
     pl.when(tm == 2)(window.start)
@@ -600,13 +606,13 @@
         start(layer_copy(2), along)
         cross(0).start()
         arrive(layer_copy(2), along)
+        cross(1).start()
+        cross(2).start()
         sent(smooth_copy, beside)
         solve_smooth(b)
         solve_restrict(b, put_guess(2))
         start(last_guess_copy, far)
         last_guess_copy(8).start()
-        cross(1).start()
-        cross(2).start()
 
     @pl.when(tm == 3)
     def _():
@@ -637,16 +643,13 @@
 
         solve_finish(b, put_last)
 
-    def give(z, _):
+    for z in range(4):
         for p in range(2):
             for i in range(4):
-                dealt[z, p, pl.ds(i, 4, stride=4), :] = res[z, i, p, 2:6, :]
-        low_part, high_part = join_columns(dealt[z, 0], dealt[z, 1])
+                dealt[0, z, p, pl.ds(i, 4, stride=4), :] = res[z, i, p, 2:6, :]
+        low_part, high_part = join_columns(dealt[0, z, 0], dealt[0, z, 1])
         o_ref[z, :, 0:128] = low_part
         o_ref[z, :, 128:256] = high_part
-        return 0
-
-    lax.fori_loop(0, 4, give, 0)
 
     sent(state_copy)
     swap.wait_send()
@@ -695,7 +698,7 @@
         return pltpu.VMEM(shape + (8, 128), jnp.float32)
 
     dma = pltpu.SemaphoreType.DMA
-    block = pl.BlockSpec(memory_space=pl.ANY)
+    block = pl.BlockSpec(memory_space=pltpu.HBM)
     raw = (states[0], diffusivity, velocity)
     counts = (9, 8, 8, 12, 8, 24, 25, 8, 3, 5)
     out = pl.pallas_call(
@@ -728,12 +731,12 @@
             vmem(4, 4, 2),
             vmem(4, 4, 2),
             vmem(4, 4, 2),
-            pltpu.VMEM((4, 2, 16, 128), jnp.float32),
+            pltpu.VMEM((5, 4, 2, 16, 128), jnp.float32),
             dma((3,)),
         ]
         + [dma((n,)) for n in counts for _ in range(2)],
         compiler_params=pltpu.CompilerParams(
-            collective_id=0, has_side_effects=True, vmem_limit_bytes=56 * 1024 * 1024
+            collective_id=0, has_side_effects=True, vmem_limit_bytes=55168 * 1024
         ),
     )(*raw)
     return out[None]

time: 49.8 us -> 48.5 us (0.974)
  local copies, waits for them, and re-layouts: 1.47 us -> 0.63 us
    unnamed x1, local copies, waits for them, and re-layouts: 1.47 us -> 0.63 us
where the time goes in v4:
time: 48.5 us; the launch traced here: 48.4 us
  Pallas kernels  47.8 us (99%)
  local copies, waits for them, and re-layouts  0.63 us (1%)
    pallas_call x1, Pallas kernels, per_device(): pl.pallas_call(kernel, name='parareal', out_shape=jax.ShapeDtypeStruct(di...  47.8 us

profile of v4, /device:TPU:57, one launch (start us, length us, event | category | flops | bytes accessed | tf_op | source)
XLA Modules:
  0.0 48.4 jit_solution(10654677159916950065)
XLA Ops:
  0.0 47.8 %parareal.1 = f32[4,16,256]{2,1,0:T(8,128)S(1)} custom-call(f32[4,16,256]{2,1,0:T(8,128)} %bitcast.3, f32[4,16,256]{2,1,0:T(8,128)} %d_hbm.1, f32[3,4,16,256]{3,2,1,0:T(8,128)} %v_hbm.1), custom_call_target="tpu_custom_call" | custom-call | tf_op jit(solution)/shard_map/parareal/pallas_call | solution.py:704
  47.8 0.6 %copy.5 = f32[1,4,16,256]{3,2,1,0:T(8,128)} copy(f32[1,4,16,256]{3,2,1,0:T(8,128)S(1)} %bitcast.2) | data formatting | bytes 131072

commit v5 on v4

--- a/solution.py
+++ b/solution.py
@@ -34,6 +34,7 @@
     return (scales, carries, tildes)
 
 
+TWO = ((2, 0), (-2, 0))
 DIRS = ((1, 0), (-1, 0), (0, 1), (0, -1), (1, 1), (1, -1), (-1, 1), (-1, -1))
 
 
@@ -63,7 +64,7 @@
 
 def coarse_box(d, blocks):
     dz, dr = d
-    z_src, z_dst = cuts(dz, 2, 2, 2)
+    z_src, z_dst = cuts(dz, 3, 2, 2)
     every = pl.ds(0, 2)
     if dr == 0:
         return (z_src, every, pl.ds(2, 4)), (z_dst, every, pl.ds(2, 4))
@@ -240,6 +241,9 @@
         else:
             part = pl.ds(0, 1) if dr == 1 else pl.ds(3, 1)
             more.append((n, (z_src, part, both, pl.ds(near[0], 1)), (z_dst, part, both, pl.ds(near[1], 1))))
+    for n, z_src, z_dst in ((0, 4, 0), (1, 7, 11)):
+        box = (every, both, pl.ds(2, 4))
+        more.append((n, (pl.ds(z_src, 1), *box), (pl.ds(z_dst, 1), *box)))
     more_dirs = [DIRS[n] for n, _, _ in more]
 
     def more_copy(q):
@@ -259,23 +263,35 @@
         src, dst = fine_box(DIRS[n], 2, 4, (2, 4), blocks=2)
         return copy(bb.at[(0, *src)], bb.at[(0, *dst)], b_send.at[n], b_recv.at[n], (tm, z, r))
 
-    def layer_copy(k):
+    def flat_guess_copy(n):
+        z, r, _ = at(*DIRS[n])
+        z_src, z_dst = cuts(DIRS[n][0], 3, 2, 2)
+        return copy(e1.at[0, z_src], e1.at[0, z_dst], e_send.at[n], e_recv.at[n], (tm, z, r))
+
+    def far_guess_copy(k):
+        def make(n):
+            z, r, _ = at(*TWO[n])
+            z_src, z_dst = ((4, 0), (3, 7))[n]
+            box = (both, pl.ds(0, 8) if k == 0 else pl.ds(2, 4))
+            sem = 2 + 2 * k + n
+            return copy(
+                e1.at[(k, pl.ds(z_src, 1), *box)], e1.at[(k, pl.ds(z_dst, 1), *box)],
+                e_send.at[sem], e_recv.at[sem], (tm, z, r),
+            )
+
+        return make
+
+    def smooth_layer_copy(k):
         def make(n):
             z, r, _ = at(*DIRS[n])
-            z_src, z_dst = cuts(DIRS[n][0], 4, 4, 2)
-            box = (every, both, pl.ds(1, 6))
-            sem = 8 * k + n
+            box = (every, both, pl.ds(0, 8) if k == 0 else pl.ds(1, 6))
+            sem = 4 + 2 * k + n
             return copy(
-                bb.at[(k, z_src, *box)], bb.at[(k, z_dst, *box)], b_send.at[sem], b_recv.at[sem],
-                (tm, z, r),
+                v1.at[(pl.ds(5, 2), *box)], vr.at[(k, pl.ds((1, 9)[n], 2), *box)],
+                r_send.at[sem], r_recv.at[sem], (tm, z, r),
             )
 
         return make
-
-    def flat_guess_copy(n):
-        z, r, _ = at(*DIRS[n])
-        z_src, z_dst = cuts(DIRS[n][0], 2, 2, 2)
-        return copy(e1.at[0, z_src], e1.at[0, z_dst], e_send.at[n], e_recv.at[n], (tm, z, r))
 
     def guess_copy(n):
         z, r, _ = at(*DIRS[n])
@@ -286,7 +302,7 @@
 
     def last_guess_copy(n):
         if n == 8:
-            box = (2, pl.ds(2, 2), both, pl.ds(2, 4))
+            box = (2, pl.ds(3, 2), both, pl.ds(2, 4))
             return copy(e1.at[box], e1.at[box], e_send.at[24], e_recv.at[24], (across, *here))
         z, r, _ = at(*DIRS[n])
         src, dst = coarse_box(DIRS[n], 1)
@@ -297,17 +313,17 @@
     def smooth_copy(n):
         z, r, _ = at(*DIRS[n])
         s_src, s_dst = (5, 1) if DIRS[n][1] == 1 else (2, 6)
-        box = (pl.ds(3, 6), pl.ds(1, 2), both)
+        box = (pl.ds(3, 6), pl.ds(1 if DIRS[n][1] == 1 else 0, 3), both)
         return copy(
-            v1.at[(*box, pl.ds(s_src, 1))], vr.at[(*box, pl.ds(s_dst, 1))],
+            v1.at[(*box, pl.ds(s_src, 1))], vr.at[(1, *box, pl.ds(s_dst, 1))],
             r_send.at[n], r_recv.at[n], (tm, z, r),
         )
 
     def jump_copy(field, n):
         z, r, _ = at(*DIRS[n])
-        src, dst = fine_box(DIRS[n], 4, 2, (1, 1))
+        src, dst = fine_box(DIRS[n], 2, 2, (1, 1))
         return lambda target: copy(
-            field.at[src], jj.at[(target, *dst)], r_send.at[n - 2], r_recv.at[n - 2 + 4 * target],
+            field.at[src], jj.at[(target, *dst)], r_send.at[n + 8], r_recv.at[n + 8 + 8 * target],
             ((sibling, z, r) if target == 0 else (tm, z, r)),
         )
 
@@ -353,7 +369,7 @@
 
         lax.fori_loop(low, high, wrapped, 0, unroll=unroll)
 
-    for edge, begin, begin_coarse in ((slab == 0, 0, 0), (slab == slabs - 1, 8, 4)):
+    for edge, begin, begin_coarse in ((slab == 0, 0, 0), (slab == slabs - 1, 8, 5)):
 
         @pl.when(edge)
         def _():
@@ -361,13 +377,26 @@
                 for m in range(4):
                     co[m, z] = zero(8)
                     cw[m, z] = zero(8)
-                for field in (sa, sb, bb.at[0], bb.at[1], bb.at[2]):
+                for field in (sa, sb, bb.at[0], vr.at[0], vr.at[1]):
                     field[z] = zero(8)
 
             loop(begin, begin + 4, clear)
             for k in range(3):
-                for z in range(begin_coarse, begin_coarse + 2):
+                for z in range(begin_coarse, begin_coarse + 3):
                     e1[k, z] = jnp.zeros((2, 8, 128), jnp.float32)
+            for k in range(2):
+
+                @pl.when(tm == 1 + 2 * k)
+                def _():
+                    for z in (2, 3) if begin == 0 else (8, 9):
+                        jj[k, z] = zero(8)
+
+    for edge, z in ((slab == 1, 0), (slab == slabs - 2, 7)):
+
+        @pl.when(edge)
+        def _():
+            for k in range(2):
+                e1[k, z] = jnp.zeros((2, 8, 128), jnp.float32)
 
     for edge, begin in ((coarse == 0, 0), (coarse == coarses - 1, 6)):
 
@@ -379,19 +408,21 @@
                 for m in range(4):
                     co[m, z, :, :, s, :] = zero(2)
                     cw[m, z, :, :, s, :] = zero(2)
-                for field in (sa, sb, bb.at[0], vr):
+                for field in (sa, sb, bb.at[0]):
                     field[z, :, :, s, :] = zero(2)
 
             loop(0, 12, clear)
+            for z in range(3, 9):
+                vr[1, z, :, :, s, :] = zero(2)
             for k in range(2):
 
                 @pl.when(tm == 1 + 2 * k)
                 def _():
-                    for z in range(4, 8):
+                    for z in range(2, 10):
                         jj[k, z, :, :, s, :] = zero(2)
 
             for k in (1, 2):
-                for z in range(6):
+                for z in range(8):
                     e1[k, z, :, s, :] = jnp.zeros((2, 2, 128), jnp.float32)
 
     arrive(state_copy)
@@ -458,7 +489,7 @@
 
     def coarse_weigh(q):
         for m in range(4):
-            mean = halves(co[m, 2 * q] + co[m, 2 * q + 1])
+            mean = halves(co[m, 2 * q - 2] + co[m, 2 * q - 1])
             cco[m, q] = mean
             if m == 0:
                 cweight[q] = RELAX / (1.0 + 3.0 * mean)
@@ -474,29 +505,28 @@
             body(z)
 
     def weights():
-        loop(3, 9, weigh)
-        loop(1, 5, coarse_weigh)
+        loop(2, 10, weigh)
+        loop(1, 7, coarse_weigh)
 
     ends = copy(fe, fx, m_send.at[1], m_recv.at[1], (sibling, *here))
     ends_first = copy(fe, res, m_send.at[1], m_recv.at[1], (sibling, *here))
     jump = copy(
         jo.at[own_box(4)], jj.at[(0, *own_box(4))], m_send.at[2], m_recv.at[2], (sibling, *here)
     )
-    jump_box = (1, pl.ds(4, 4), every, both, pl.ds(1, 6))
+    jump_box = (1, pl.ds(2, 8), every, both, pl.ds(1, 6))
     last_jump = copy(jj.at[jump_box], jj.at[jump_box], m_send.at[4], m_recv.at[4], (across, *here))
     third = copy(res, res, m_send.at[3], m_recv.at[3], (sibling, *here))
-    cross_boxes = [(2, pl.ds(low, n), every, both, pl.ds(1, 6)) for low, n in ((4, 4), (2, 2), (8, 2))]
-
-    def cross(n):
-        box = cross_boxes[n]
-        return copy(bb.at[box], bb.at[box], x_send.at[n], x_recv.at[n], (across, *here))
+    cross_box = (2, pl.ds(2, 8), every, both, pl.ds(1, 6))
+    cross = copy(
+        bb.at[cross_box], bb.at[cross_box], x_send.at[0], x_recv.at[0], (across, *here)
+    )
 
     @pl.when(tm == 0)
     def _():
         window.wait_recv()
         for z in range(4):
             jo[z + 4] = fe[z] - sx[z]
-        start(lambda n: jump_copy(jo, n)(0), beside)
+        start(lambda n: jump_copy(jo, n)(0), far)
         jump.start()
         ends.start()
         ends_first.wait_recv()
@@ -516,30 +546,29 @@
     def solve_restrict(b, put):
         def restrict(q):
             total = None
-            for z in (2 * q, 2 * q + 1):
+            for z in (2 * q - 2, 2 * q - 1):
                 centre, spread, drift = operator(v1, co, z)
                 misfit = b[z] - centre + 2.0 * (spread - drift)
                 total = misfit if total is None else total + misfit
             put(q, cweight[q] * halves(total))
 
-        loop(2, 4, restrict)
-
-    def solve_correct(e, base):
-        def correct(q):
+        loop(3, 5, restrict)
+
+    def solve_correct(e, base, reach):
+        for q in range(3 - reach, 5 + reach):
             centre, spread, drift = operator(e, cco, q, fine=False)
             w = cweight[q]
             wide = spread_out((2.0 - w) * centre + w * (0.5 * spread - drift))
-            for z in (2 * q, 2 * q + 1):
-                v2[z] = base(z) + wide
-
-        loop(1, 5, correct)
-
-    def solve_finish(b, put):
+            for z in (2 * q - 2, 2 * q - 1):
+                if z >= 4 - 2 * reach + (reach - 1) and z < 8 + 2 * reach - (reach - 1):
+                    v2[z] = base(z) + wide
+
+    def solve_finish(b, put, reach):
         def finish(z):
             centre, spread, drift = operator(v2, co, z)
             put(z, centre + weight[z] * (b[z] - centre + 2.0 * (spread - drift)))
 
-        loop(4, 8, finish)
+        loop(4 - reach, 8 + reach, finish)
 
     def put_guess(k):
         def put(q, value):
@@ -558,57 +587,68 @@
         merge(4, 8, pl.ds(0, 1), pl.ds(3, 1))
         for z in (3, 8):
             merge(z, z + 1, pl.ds(0, 2), pl.ds(2, 2))
+        for z in (0, 11):
+            for m in range(4):
+                co[m, z, :, :, 2:6, :] = cw[m, z, :, :, 2:6, :]
         weights()
         arrive(first_copy)
         solve_smooth(b)
+        start(smooth_layer_copy(0), along)
 
         def put_flat(q, value):
             e1[0, q] = value
 
         solve_restrict(b, put_flat)
+        start(far_guess_copy(0), along, TWO)
         start(flat_guess_copy, along)
+        arrive(smooth_layer_copy(0), along)
         arrive(flat_guess_copy, along)
-        solve_correct(e1.at[0], lambda z: v1[z])
-        arrive(lambda n: jump_copy(jo, n)(0), beside)
+        arrive(far_guess_copy(0), along, TWO)
+        solve_correct(e1.at[0], lambda z: v1[z] if 3 <= z < 9 else vr[0, z], 2)
+        arrive(lambda n: jump_copy(jo, n)(0))
         jump.wait_recv()
         b = bb.at[1]
 
         def put_first(z, value):
             bb[1, z] = value + jj[0, z]
-            xout[z - 4] = value
-
-        solve_finish(bb.at[0], put_first)
-        start(layer_copy(1), along)
+
+        solve_finish(bb.at[0], put_first, 2)
+
+        sent(smooth_layer_copy(0), along)
+        solve_smooth(b)
+        start(smooth_copy, beside)
+        start(smooth_layer_copy(1), along)
+        solve_restrict(b, put_guess(1))
+        start(guess_copy, (4, 5, 6, 7, 2, 3))
+        start(far_guess_copy(1), along, TWO)
+        start(guess_copy, along)
         ends.wait_recv()
         for z in range(4):
-            res[z] = fx[z] + xout[z]
-
-        arrive(layer_copy(1), along)
-        solve_smooth(b)
-        start(smooth_copy, beside)
-        solve_restrict(b, put_guess(1))
-        start(guess_copy, far)
+            res[z] = fx[z] + (b[z + 4] - jj[0, z + 4])
         shape = (4, 2, 8, 128)
         i = lax.broadcasted_iota(jnp.int32, shape, 0)
         sub = lax.broadcasted_iota(jnp.int32, shape, 2)
-        given = ((sub == 1) | (sub == 6)) & ((i == 1) | (i == 2))
+        given = ((sub == 1) & (i > 0)) | ((sub == 6) & (i < 3))
         arrive(smooth_copy, beside)
+        arrive(smooth_layer_copy(1), along)
         arrive(guess_copy)
-        solve_correct(e1.at[1], lambda z: jnp.where(given, vr[z], v1[z]))
+        arrive(far_guess_copy(1), along, TWO)
+        solve_correct(
+            e1.at[1],
+            lambda z: jnp.where(given, vr[1, z], v1[z]) if 3 <= z < 9 else vr[1, z],
+            2,
+        )
         last_jump.wait_recv()
 
         def put_second(z, value):
             bb[2, z] = value + jj[1, z]
 
-        solve_finish(b, put_second)
+        solve_finish(b, put_second, 2)
 
         b = bb.at[2]
-        start(layer_copy(2), along)
-        cross(0).start()
-        arrive(layer_copy(2), along)
-        cross(1).start()
-        cross(2).start()
+        cross.start()
         sent(smooth_copy, beside)
+        sent(smooth_layer_copy(1), along)
         solve_smooth(b)
         solve_restrict(b, put_guess(2))
         start(last_guess_copy, far)
@@ -620,28 +660,26 @@
             value = fe[z] - own[z]
             jo[z + 4] = value
             to_own_rows(jj.at[1], z + 4, value)
-        start(lambda n: jump_copy(jo, n)(1), beside)
+        start(lambda n: jump_copy(jo, n)(1), far)
         weights()
-        arrive(lambda n: jump_copy(jo, n)(1), beside)
+        arrive(lambda n: jump_copy(jo, n)(1))
         last_jump.start()
         b = bb.at[2]
-        cross(0).wait_recv()
+        cross.wait_recv()
         for z in range(4):
             res[z] = b[z + 4] + own[z]
         third.start()
-        cross(1).wait_recv()
-        cross(2).wait_recv()
         solve_smooth(b)
         arrive(last_guess_copy)
         last_guess_copy(8).wait_recv()
-        solve_correct(e1.at[2], lambda z: v1[z])
+        solve_correct(e1.at[2], lambda z: v1[z], 1)
         ends.wait_recv()
         third.wait_send()
 
         def put_last(z, value):
             res[z - 4] = fx[z - 4] + value
 
-        solve_finish(b, put_last)
+        solve_finish(b, put_last, 0)
 
     for z in range(4):
         for p in range(2):
@@ -664,7 +702,7 @@
 
     @pl.when(tm == 0)
     def _():
-        sent(lambda n: jump_copy(jo, n)(0), beside)
+        sent(lambda n: jump_copy(jo, n)(0))
         jump.wait_send()
         ends.wait_send()
 
@@ -679,17 +717,16 @@
         sent(first_copy)
         ends_first.wait_send()
         sent(flat_guess_copy, along)
-        sent(layer_copy(1), along)
+        sent(far_guess_copy(0), along, TWO)
         sent(guess_copy)
-        sent(layer_copy(2), along)
+        sent(far_guess_copy(1), along, TWO)
         sent(last_guess_copy)
         last_guess_copy(8).wait_send()
-        for n in range(3):
-            cross(n).wait_send()
+        cross.wait_send()
 
     @pl.when(tm == 3)
     def _():
-        sent(lambda n: jump_copy(jo, n)(1), beside)
+        sent(lambda n: jump_copy(jo, n)(1))
         last_jump.wait_send()
 
 
@@ -700,7 +737,7 @@
     dma = pltpu.SemaphoreType.DMA
     block = pl.BlockSpec(memory_space=pltpu.HBM)
     raw = (states[0], diffusivity, velocity)
-    counts = (9, 8, 8, 12, 8, 24, 25, 8, 3, 5)
+    counts = (9, 8, 8, 14, 8, 8, 25, 24, 1, 5)
     out = pl.pallas_call(
         kernel,
         name="parareal",
@@ -723,10 +760,10 @@
             vmem(3, 12, 4, 2),
             vmem(12, 4, 2),
             vmem(12, 4, 2),
-            vmem(12, 4, 2),
-            vmem(3, 6, 2),
-            vmem(4, 6, 2),
-            vmem(6, 2),
+            vmem(2, 12, 4, 2),
+            vmem(3, 8, 2),
+            vmem(4, 8, 2),
+            vmem(8, 2),
             vmem(4, 4, 2),
             vmem(4, 4, 2),
             vmem(4, 4, 2),

time: 48.5 us -> 47.2 us (0.973)
  the two profiles are of different devices: /device:TPU:57 before, /device:TPU:51 now
where the time goes in v5:
time: 47.2 us; the launch traced here: 47 us
  Pallas kernels  46.4 us (98%)
  local copies, waits for them, and re-layouts  0.63 us (1%)
    pallas_call x1, Pallas kernels, per_device(): pl.pallas_call(kernel, name='parareal', out_shape=jax.ShapeDtypeStruct(di...  46.4 us

profile of v5, /device:TPU:51, one launch (start us, length us, event | category | flops | bytes accessed | tf_op | source)
XLA Modules:
  0.0 47.0 jit_solution(14895345027416577565)
XLA Ops:
  0.0 46.4 %parareal.1 = f32[4,16,256]{2,1,0:T(8,128)S(1)} custom-call(f32[4,16,256]{2,1,0:T(8,128)} %bitcast.3, f32[4,16,256]{2,1,0:T(8,128)} %d_hbm.1, f32[3,4,16,256]{3,2,1,0:T(8,128)} %v_hbm.1), custom_call_target="tpu_custom_call" | custom-call | tf_op jit(solution)/shard_map/parareal/pallas_call | solution.py:741
  46.4 0.6 %copy.5 = f32[1,4,16,256]{3,2,1,0:T(8,128)} copy(f32[1,4,16,256]{3,2,1,0:T(8,128)S(1)} %bitcast.2) | data formatting | bytes 131072

commit v6 on v5

--- a/solution.py
+++ b/solution.py
@@ -284,7 +284,7 @@
     def smooth_layer_copy(k):
         def make(n):
             z, r, _ = at(*DIRS[n])
-            box = (every, both, pl.ds(0, 8) if k == 0 else pl.ds(1, 6))
+            box = (every, both, pl.ds(1, 6))
             sem = 4 + 2 * k + n
             return copy(
                 v1.at[(pl.ds(5, 2), *box)], vr.at[(k, pl.ds((1, 9)[n], 2), *box)],
@@ -516,10 +516,15 @@
     jump_box = (1, pl.ds(2, 8), every, both, pl.ds(1, 6))
     last_jump = copy(jj.at[jump_box], jj.at[jump_box], m_send.at[4], m_recv.at[4], (across, *here))
     third = copy(res, res, m_send.at[3], m_recv.at[3], (sibling, *here))
-    cross_box = (2, pl.ds(2, 8), every, both, pl.ds(1, 6))
-    cross = copy(
-        bb.at[cross_box], bb.at[cross_box], x_send.at[0], x_recv.at[0], (across, *here)
+    cross_boxes = (
+        (2, pl.ds(2, 8), every, both, pl.ds(2, 4)),
+        (2, pl.ds(3, 6), pl.ds(2, 2), both, pl.ds(1, 1)),
+        (2, pl.ds(3, 6), pl.ds(0, 2), both, pl.ds(6, 1)),
     )
+    cross = [
+        copy(bb.at[box], bb.at[box], x_send.at[n], x_recv.at[n], (across, *here))
+        for n, box in enumerate(cross_boxes)
+    ]
 
     @pl.when(tm == 0)
     def _():
@@ -646,7 +651,8 @@
         solve_finish(b, put_second, 2)
 
         b = bb.at[2]
-        cross.start()
+        for part in cross:
+            part.start()
         sent(smooth_copy, beside)
         sent(smooth_layer_copy(1), along)
         solve_smooth(b)
@@ -665,7 +671,8 @@
         arrive(lambda n: jump_copy(jo, n)(1))
         last_jump.start()
         b = bb.at[2]
-        cross.wait_recv()
+        for part in cross:
+            part.wait_recv()
         for z in range(4):
             res[z] = b[z + 4] + own[z]
         third.start()
@@ -722,7 +729,8 @@
         sent(far_guess_copy(1), along, TWO)
         sent(last_guess_copy)
         last_guess_copy(8).wait_send()
-        cross.wait_send()
+        for part in cross:
+            part.wait_send()
 
     @pl.when(tm == 3)
     def _():
@@ -737,7 +745,7 @@
     dma = pltpu.SemaphoreType.DMA
     block = pl.BlockSpec(memory_space=pltpu.HBM)
     raw = (states[0], diffusivity, velocity)
-    counts = (9, 8, 8, 14, 8, 8, 25, 24, 1, 5)
+    counts = (9, 8, 8, 14, 8, 8, 25, 24, 3, 5)
     out = pl.pallas_call(
         kernel,
         name="parareal",

time: 47.2 us -> 46.2 us (0.979)
  Pallas kernels: 46.4 us -> 45.4 us
    pallas_call x1, Pallas kernels: 46.4 us -> 45.4 us  [per_device(): pl.pallas_call(kernel, name='parareal', out_shape=jax.ShapeDtypeStruct(di...]
where the time goes in v6:
time: 46.2 us; the launch traced here: 46 us
  Pallas kernels  45.4 us (98%)
  local copies, waits for them, and re-layouts  0.63 us (1%)
    pallas_call x1, Pallas kernels, per_device(): pl.pallas_call(kernel, name='parareal', out_shape=jax.ShapeDtypeStruct(di...  45.4 us

profile of v6, /device:TPU:51, one launch (start us, length us, event | category | flops | bytes accessed | tf_op | source)
XLA Modules:
  0.0 46.0 jit_solution(13083522854627678533)
XLA Ops:
  0.0 45.4 %parareal.1 = f32[4,16,256]{2,1,0:T(8,128)S(1)} custom-call(f32[4,16,256]{2,1,0:T(8,128)} %bitcast.3, f32[4,16,256]{2,1,0:T(8,128)} %d_hbm.1, f32[3,4,16,256]{3,2,1,0:T(8,128)} %v_hbm.1), custom_call_target="tpu_custom_call" | custom-call | tf_op jit(solution)/shard_map/parareal/pallas_call | solution.py:749
  45.4 0.6 %copy.5 = f32[1,4,16,256]{3,2,1,0:T(8,128)} copy(f32[1,4,16,256]{3,2,1,0:T(8,128)S(1)} %bitcast.2) | data formatting | bytes 131072

commit v7 on v6

--- a/solution.py
+++ b/solution.py
@@ -517,9 +517,11 @@
     last_jump = copy(jj.at[jump_box], jj.at[jump_box], m_send.at[4], m_recv.at[4], (across, *here))
     third = copy(res, res, m_send.at[3], m_recv.at[3], (sibling, *here))
     cross_boxes = (
-        (2, pl.ds(2, 8), every, both, pl.ds(2, 4)),
+        (2, pl.ds(3, 6), every, both, pl.ds(2, 4)),
         (2, pl.ds(3, 6), pl.ds(2, 2), both, pl.ds(1, 1)),
         (2, pl.ds(3, 6), pl.ds(0, 2), both, pl.ds(6, 1)),
+        (2, pl.ds(2, 1), every, both, pl.ds(2, 4)),
+        (2, pl.ds(9, 1), every, both, pl.ds(2, 4)),
     )
     cross = [
         copy(bb.at[box], bb.at[box], x_send.at[n], x_recv.at[n], (across, *here))
@@ -541,12 +543,13 @@
         ends.start()
         third.wait_recv()
 
-    def solve_smooth(b):
+    def solve_smooth(b, spans=((3, 9),)):
         def smooth(z):
             centre, spread, drift = operator(b, co, z)
             v1[z] = centre + (2.0 * weight[z]) * (spread - drift)
 
-        loop(3, 9, smooth)
+        for low, high in spans:
+            loop(low, high, smooth)
 
     def solve_restrict(b, put):
         def restrict(q):
@@ -671,12 +674,15 @@
         arrive(lambda n: jump_copy(jo, n)(1))
         last_jump.start()
         b = bb.at[2]
-        for part in cross:
+        for part in cross[:3]:
             part.wait_recv()
         for z in range(4):
             res[z] = b[z + 4] + own[z]
         third.start()
-        solve_smooth(b)
+        solve_smooth(b, ((4, 8),))
+        for part in cross[3:]:
+            part.wait_recv()
+        solve_smooth(b, ((3, 4), (8, 9)))
         arrive(last_guess_copy)
         last_guess_copy(8).wait_recv()
         solve_correct(e1.at[2], lambda z: v1[z], 1)
@@ -745,7 +751,7 @@
     dma = pltpu.SemaphoreType.DMA
     block = pl.BlockSpec(memory_space=pltpu.HBM)
     raw = (states[0], diffusivity, velocity)
-    counts = (9, 8, 8, 14, 8, 8, 25, 24, 3, 5)
+    counts = (9, 8, 8, 14, 8, 8, 25, 24, 5, 5)
     out = pl.pallas_call(
         kernel,
         name="parareal",

time: 46.2 us -> 46.2 us (level)
  no operation moved by 1% of the time
where the time goes in v7:
time: 46.2 us; the launch traced here: 46.1 us
  Pallas kernels  45.4 us (98%)
  local copies, waits for them, and re-layouts  0.63 us (1%)
    pallas_call x1, Pallas kernels, per_device(): pl.pallas_call(kernel, name='parareal', out_shape=jax.ShapeDtypeStruct(di...  45.4 us

profile of v7, /device:TPU:51, one launch (start us, length us, event | category | flops | bytes accessed | tf_op | source)
XLA Modules:
  0.0 46.1 jit_solution(18100808594323856790)
XLA Ops:
  0.0 45.4 %parareal.1 = f32[4,16,256]{2,1,0:T(8,128)S(1)} custom-call(f32[4,16,256]{2,1,0:T(8,128)} %bitcast.3, f32[4,16,256]{2,1,0:T(8,128)} %d_hbm.1, f32[3,4,16,256]{3,2,1,0:T(8,128)} %v_hbm.1), custom_call_target="tpu_custom_call" | custom-call | tf_op jit(solution)/shard_map/parareal/pallas_call | solution.py:755
  45.5 0.6 %copy.5 = f32[1,4,16,256]{3,2,1,0:T(8,128)} copy(f32[1,4,16,256]{3,2,1,0:T(8,128)S(1)} %bitcast.2) | data formatting | bytes 131072

commit v8 on v6

--- a/solution.py
+++ b/solution.py
@@ -516,14 +516,10 @@
     jump_box = (1, pl.ds(2, 8), every, both, pl.ds(1, 6))
     last_jump = copy(jj.at[jump_box], jj.at[jump_box], m_send.at[4], m_recv.at[4], (across, *here))
     third = copy(res, res, m_send.at[3], m_recv.at[3], (sibling, *here))
-    cross_boxes = (
-        (2, pl.ds(2, 8), every, both, pl.ds(2, 4)),
-        (2, pl.ds(3, 6), pl.ds(2, 2), both, pl.ds(1, 1)),
-        (2, pl.ds(3, 6), pl.ds(0, 2), both, pl.ds(6, 1)),
-    )
+    cross_box = (2, *own_box(4))
     cross = [
-        copy(bb.at[box], bb.at[box], x_send.at[n], x_recv.at[n], (across, *here))
-        for n, box in enumerate(cross_boxes)
+        copy(a.at[box], a.at[box], x_send.at[n], x_recv.at[n], (across, *here))
+        for n, (a, box) in enumerate(((bb, cross_box), (xout, own_box(0))))
     ]
 
     @pl.when(tm == 0)
@@ -548,12 +544,14 @@
 
         loop(3, 9, smooth)
 
-    def solve_restrict(b, put):
+    def solve_restrict(b, put, keep=False):
         def restrict(q):
             total = None
             for z in (2 * q - 2, 2 * q - 1):
                 centre, spread, drift = operator(v1, co, z)
                 misfit = b[z] - centre + 2.0 * (spread - drift)
+                if keep:
+                    xout[z - 4] = centre + weight[z] * misfit
                 total = misfit if total is None else total + misfit
             put(q, cweight[q] * halves(total))
 
@@ -651,14 +649,14 @@
         solve_finish(b, put_second, 2)
 
         b = bb.at[2]
-        for part in cross:
-            part.start()
+        cross[0].start()
         sent(smooth_copy, beside)
         sent(smooth_layer_copy(1), along)
         solve_smooth(b)
-        solve_restrict(b, put_guess(2))
+        solve_restrict(b, put_guess(2), keep=True)
         start(last_guess_copy, far)
         last_guess_copy(8).start()
+        cross[1].start()
 
     @pl.when(tm == 3)
     def _():
@@ -671,22 +669,20 @@
         arrive(lambda n: jump_copy(jo, n)(1))
         last_jump.start()
         b = bb.at[2]
-        for part in cross:
-            part.wait_recv()
+        cross[0].wait_recv()
         for z in range(4):
             res[z] = b[z + 4] + own[z]
         third.start()
-        solve_smooth(b)
         arrive(last_guess_copy)
         last_guess_copy(8).wait_recv()
-        solve_correct(e1.at[2], lambda z: v1[z], 1)
+        solve_correct(e1.at[2], lambda z: 0.0, 1)
         ends.wait_recv()
+        cross[1].wait_recv()
         third.wait_send()
-
-        def put_last(z, value):
-            res[z - 4] = fx[z - 4] + value
-
-        solve_finish(b, put_last, 0)
+        for z in range(4, 8):
+            centre, spread, drift = operator(v2, co, z)
+            change = centre + weight[z] * (2.0 * (spread - drift) - centre)
+            res[z - 4] = fx[z - 4] + xout[z - 4] + change
 
     for z in range(4):
         for p in range(2):

time: 46.2 us -> 44.9 us (0.972)
  the two profiles are of different devices: /device:TPU:51 before, /device:TPU:57 now
where the time goes in v8:
time: 44.9 us; the launch traced here: 44.2 us
  Pallas kernels  43.6 us (97%)
  local copies, waits for them, and re-layouts  0.63 us (1%)
    pallas_call x1, Pallas kernels, per_device(): pl.pallas_call(kernel, name='parareal', out_shape=jax.ShapeDtypeStruct(di...  43.6 us

profile of v8, /device:TPU:57, one launch (start us, length us, event | category | flops | bytes accessed | tf_op | source)
XLA Modules:
  0.0 44.2 jit_solution(13396598051589123884)
XLA Ops:
  0.0 43.6 %parareal.1 = f32[4,16,256]{2,1,0:T(8,128)S(1)} custom-call(f32[4,16,256]{2,1,0:T(8,128)} %bitcast.3, f32[4,16,256]{2,1,0:T(8,128)} %d_hbm.1, f32[3,4,16,256]{3,2,1,0:T(8,128)} %v_hbm.1), custom_call_target="tpu_custom_call" | custom-call | tf_op jit(solution)/shard_map/parareal/pallas_call | solution.py:745
  43.6 0.6 %copy.5 = f32[1,4,16,256]{3,2,1,0:T(8,128)} copy(f32[1,4,16,256]{3,2,1,0:T(8,128)S(1)} %bitcast.2) | data formatting | bytes 131072
